TPU v7x, 32 devices: a whole 2x2x4 slice. The times are simulated.
32 devices in a mesh: seq: 8 (over z, core), batch: 4 (over y, x).
Axes of the slice: x: 2, y: 2, z: 4, core: 2. Of those that a mesh axis runs over, the one named last changes fastest.
Arguments:
- layer_inputs: bfloat16 [16, 2048, 768], P('batch', 'seq'), may hold values from -6 to 6
- document_openings: int32 [16, 2048], P('batch', 'seq'), may hold values from 0 to 1, as said below
- mixing_lookup_projection: bfloat16 [768, 768], P(('seq', 'batch')), may hold values from -0.21875 to 0.21875
- mixing_payload_projection: bfloat16 [768, 768], P(('seq', 'batch')), may hold values from -0.21875 to 0.21875
- mixing_acceptor_projection: bfloat16 [768, 768], P(('seq', 'batch')), may hold values from -0.21875 to 0.21875
- mixing_result_projection: bfloat16 [768, 768], P(('seq', 'batch')), may hold values from -0.875 to 0.875
- feedforward_lookup_projection: bfloat16 [768, 3072], P(('seq', 'batch')), may hold values from -0.21875 to 0.21875
- feedforward_acceptor_projection: bfloat16 [768, 768], P(('seq', 'batch')), may hold values from -0.21875 to 0.21875
- feedforward_payload_projection: bfloat16 [3072, 768], P(('seq', 'batch')), may hold values from -0.15625 to 0.15625
- premix_layer_scaling: bfloat16 [768], P(('seq', 'batch')), may hold values from 0.25 to 1.75
- premix_layer_offset: bfloat16 [768], P(('seq', 'batch')), may hold values from -3 to 3
- postmix_layer_scaling: bfloat16 [768], P(('seq', 'batch')), may hold values from 0.25 to 1.75
- postmix_layer_offset: bfloat16 [768], P(('seq', 'batch')), may hold values from -3 to 3
- mixing_lookup_blend: bfloat16 [768], P(('seq', 'batch')), may hold values from 0.049804688 to 0.94921875
- mixing_payload_blend: bfloat16 [768], P(('seq', 'batch')), may hold values from 0.049804688 to 0.94921875
- mixing_acceptor_blend: bfloat16 [768], P(('seq', 'batch')), may hold values from 0.049804688 to 0.94921875
- feedforward_lookup_blend: bfloat16 [768], P(('seq', 'batch')), may hold values from 0.049804688 to 0.94921875
- feedforward_acceptor_blend: bfloat16 [768], P(('seq', 'batch')), may hold values from 0.049804688 to 0.94921875
- feature_fading_speed: bfloat16 [768], P(('seq', 'batch')), may hold values from 9.765625e-05 to 0.08, as said below
- present_token_reward: bfloat16 [768], P(('seq', 'batch')), may hold values from -1 to 1
- upstream_adjoint: bfloat16 [16, 2048, 768], P('batch', 'seq'), may hold values from -6 to 6
Outputs:
- block_out: bfloat16 [16, 2048, 768], P('batch', 'seq')
- tokens_grad: float32 [16, 2048, 768], P('batch', 'seq')
- key_weight_grad: float32 [768, 768], P(('seq', 'batch'))
- value_weight_grad: float32 [768, 768], P(('seq', 'batch'))
- gate_weight_grad: float32 [768, 768], P(('seq', 'batch'))
- output_weight_grad: float32 [768, 768], P(('seq', 'batch'))
- expand_weight_grad: float32 [768, 3072], P(('seq', 'batch'))
- select_weight_grad: float32 [768, 768], P(('seq', 'batch'))
- contract_weight_grad: float32 [3072, 768], P(('seq', 'batch'))
- attn_gain_grad: float32 [768], P(('seq', 'batch'))
- attn_bias_grad: float32 [768], P(('seq', 'batch'))
- chan_gain_grad: float32 [768], P(('seq', 'batch'))
- chan_bias_grad: float32 [768], P(('seq', 'batch'))
- key_ratio_grad: float32 [768], P(('seq', 'batch'))
- value_ratio_grad: float32 [768], P(('seq', 'batch'))
- gate_ratio_grad: float32 [768], P(('seq', 'batch'))
- expand_ratio_grad: float32 [768], P(('seq', 'batch'))
- select_ratio_grad: float32 [768], P(('seq', 'batch'))
- decay_rate_grad: float32 [768], P(('seq', 'batch'))
- bonus_term_grad: float32 [768], P(('seq', 'batch'))
Inputs may be any that keep to these rules, and one draw needn't show every extreme that they name: `document_openings`: 1 marks a token that begins a document; in each aligned group of 4 sequences one sequence, drawn from the seed, holds no 1 at all. `feature_fading_speed`: positive per-channel rates.
All inputs are finite; a program needn't handle non-finite values.
Results may differ from a plain program's by a relative error of at most 0.013.
Values may be sent and summed in bfloat16 or wider, within the bound.
A program may use at most 256 MiB of HBM per device.

v0:
```python
import jax
import jax.numpy as jnp
from jax import lax
from jax.sharding import PartitionSpec as P

EPSILON = 1e-05


def from_behind(block, axis, distance):
    devices = range(lax.axis_size(axis))
    route = [(i - distance, i) for i in devices if i - distance in devices]
    return lax.ppermute(block, axis, route)


def prefix(part, axis, combine, identity, reverse):
    count = lax.axis_size(axis)
    place = lax.axis_index(axis)
    ahead = count - 1 - place if reverse else place
    gathered = jax.tree.map(lambda a: lax.all_gather(a, axis), part)
    state = jax.tree.map(lambda a, e: jnp.zeros_like(a) + jnp.asarray(e, a.dtype), part, identity)

    def one(turn, state):
        source = count - 1 - turn if reverse else turn
        return combine(
            state, jax.tree.map(lambda a: lax.dynamic_index_in_dim(a, source, 0, False), gathered)
        )

    return lax.fori_loop(0, ahead, one, state)


def layer_norm(values, gain, offset):
    center = values - jnp.mean(values, axis=-1, keepdims=True)
    factor = lax.rsqrt(jnp.mean(center * center, axis=-1, keepdims=True) + EPSILON)
    normed = center * factor
    return (normed * gain + offset, normed, factor)


def norm_back(grad_out, normed, factor, gain):
    scaled = grad_out * gain
    centered = scaled - jnp.mean(scaled, axis=-1, keepdims=True)
    grad_in = factor * (centered - normed * jnp.mean(scaled * normed, axis=-1, keepdims=True))
    return (grad_in, jnp.sum(grad_out * normed, axis=(0, 1)), jnp.sum(grad_out, axis=(0, 1)))


def product(left, right):
    return jnp.einsum("scd,de->sce", left, right, preferred_element_type=jnp.float32)


def product_back(grad, right):
    return jnp.einsum("sce,de->scd", grad, right, preferred_element_type=jnp.float32)


def outer_sum(left, grad):
    return jnp.einsum("scd,sce->de", left, grad, preferred_element_type=jnp.float32)


def attach_previous(values, arriving, persisting_indicator):
    return jnp.concatenate([arriving, values[:, :-1]], axis=1) * persisting_indicator[..., None]


def attach_next(masked, arriving):
    return jnp.concatenate([masked[:, 1:], arriving], axis=1)


def make_combine(fading_multiplier):

    def combine(earlier, later):
        early_numer, early_denom, early_length, early_cut = earlier
        late_numer, late_denom, late_length, late_cut = later
        fading = jnp.exp(-late_length * fading_multiplier) * (1.0 - late_cut)
        return (
            late_numer + fading * early_numer,
            late_denom + fading * early_denom,
            early_length + late_length,
            jnp.maximum(early_cut, late_cut),
        )

    return combine


def affine_compose(first_step, second_step):
    first_mult, first_numer, first_denom = first_step
    second_mult, second_numer, second_denom = second_step
    return (
        first_mult * second_mult,
        second_mult * first_numer + second_numer,
        second_mult * first_denom + second_denom,
    )


def forward_sweep(exponentiated_lookup, payload_table_lines, persisting_indicator, shrink):
    multiplier = persisting_indicator[..., None] * shrink
    inclusive = lax.associative_scan(
        affine_compose,
        (multiplier, exponentiated_lookup * payload_table_lines, exponentiated_lookup),
        axis=1,
    )
    zeros = jnp.zeros_like(exponentiated_lookup[:, :1])
    numer_all = (
        jnp.concatenate([zeros, inclusive[1][:, :-1]], axis=1) * persisting_indicator[..., None]
    )
    denom_all = (
        jnp.concatenate([zeros, inclusive[2][:, :-1]], axis=1) * persisting_indicator[..., None]
    )
    return (numer_all, denom_all, inclusive[1][:, -1], inclusive[2][:, -1])


def reverse_sweep(adjoint_dividend, grad_denom, persisting_indicator, shrink):
    keep_now = persisting_indicator[..., None]
    inclusive = lax.associative_scan(
        affine_compose,
        (keep_now * shrink, keep_now * adjoint_dividend, keep_now * grad_denom),
        axis=1,
        reverse=True,
    )
    zeros = jnp.zeros_like(adjoint_dividend[:, :1])
    following_dividend = jnp.concatenate([inclusive[1][:, 1:], zeros], axis=1)
    next_denom = jnp.concatenate([inclusive[2][:, 1:], zeros], axis=1)
    return (following_dividend, next_denom, inclusive[1][:, 0], inclusive[2][:, 0])


def body(
    layer_inputs,
    document_openings,
    mixing_lookup_projection,
    mixing_payload_projection,
    mixing_acceptor_projection,
    mixing_result_projection,
    feedforward_lookup_projection,
    feedforward_acceptor_projection,
    feedforward_payload_projection,
    premix_layer_scaling,
    premix_layer_offset,
    postmix_layer_scaling,
    postmix_layer_offset,
    mixing_lookup_blend,
    mixing_payload_blend,
    mixing_acceptor_blend,
    feedforward_lookup_blend,
    feedforward_acceptor_blend,
    feature_fading_speed,
    present_token_reward,
    upstream_adjoint,
):
    gathered = (
        lax.all_gather(mixing_lookup_projection, ("seq", "batch"), axis=0, tiled=True),
        lax.all_gather(mixing_payload_projection, ("seq", "batch"), axis=0, tiled=True),
        lax.all_gather(mixing_acceptor_projection, ("seq", "batch"), axis=0, tiled=True),
        lax.all_gather(mixing_result_projection, ("seq", "batch"), axis=0, tiled=True),
        lax.all_gather(feedforward_lookup_projection, ("seq", "batch"), axis=0, tiled=True),
        lax.all_gather(feedforward_acceptor_projection, ("seq", "batch"), axis=0, tiled=True),
        lax.all_gather(feedforward_payload_projection, ("seq", "batch"), axis=0, tiled=True),
        lax.all_gather(premix_layer_scaling, ("seq", "batch"), axis=0, tiled=True),
        lax.all_gather(premix_layer_offset, ("seq", "batch"), axis=0, tiled=True),
        lax.all_gather(postmix_layer_scaling, ("seq", "batch"), axis=0, tiled=True),
        lax.all_gather(postmix_layer_offset, ("seq", "batch"), axis=0, tiled=True),
        lax.all_gather(mixing_lookup_blend, ("seq", "batch"), axis=0, tiled=True),
        lax.all_gather(mixing_payload_blend, ("seq", "batch"), axis=0, tiled=True),
        lax.all_gather(mixing_acceptor_blend, ("seq", "batch"), axis=0, tiled=True),
        lax.all_gather(feedforward_lookup_blend, ("seq", "batch"), axis=0, tiled=True),
        lax.all_gather(feedforward_acceptor_blend, ("seq", "batch"), axis=0, tiled=True),
        lax.all_gather(feature_fading_speed, ("seq", "batch"), axis=0, tiled=True),
        lax.all_gather(present_token_reward, ("seq", "batch"), axis=0, tiled=True),
    )
    full_key, full_value, full_gate, full_output, full_expand, full_select, full_contract = (
        gathered[:7]
    )
    vectors = [stream_element.astype(jnp.float32) for stream_element in gathered[7:]]
    (
        gain_first,
        bias_first,
        gain_second,
        bias_second,
        ratio_key,
        ratio_value,
        ratio_gate,
        ratio_expand,
        ratio_select,
        fading_multiplier,
        present_reward_term,
    ) = vectors
    inputs = layer_inputs.astype(jnp.float32)
    flags = document_openings.astype(jnp.float32)
    persisting_indicator = 1.0 - flags
    sequences = layer_inputs.shape[0]
    block_len = layer_inputs.shape[1]
    width = layer_inputs.shape[2]
    normed_a, unit_a, factor_a = layer_norm(inputs, gain_first, bias_first)
    arriving_a = from_behind(normed_a[:, -1:, :], "seq", 1)
    before_a = attach_previous(normed_a, arriving_a, persisting_indicator)
    spread_a = normed_a - before_a
    key_in = (before_a + spread_a * ratio_key).astype(jnp.bfloat16)
    value_in = (before_a + spread_a * ratio_value).astype(jnp.bfloat16)
    gate_in = (before_a + spread_a * ratio_gate).astype(jnp.bfloat16)
    lookup_table_lines = product(key_in, full_key)
    payload_table_lines = product(value_in, full_value)
    gate_rows = product(gate_in, full_gate)
    shrink = jnp.exp(-fading_multiplier)
    exponentiated_lookup = jnp.exp(lookup_table_lines)
    reward_scaled_pairs = jnp.exp(present_reward_term + lookup_table_lines)
    local_numer, local_denom, end_numer, end_denom = forward_sweep(
        exponentiated_lookup, payload_table_lines, persisting_indicator, shrink
    )
    cut = jnp.max(flags, axis=1, keepdims=True)
    length = jnp.full((1,), float(block_len), jnp.float32)
    zero_state = jnp.zeros((sequences, width), jnp.float32)
    identity = (
        zero_state,
        zero_state,
        jnp.zeros((1,), jnp.float32),
        jnp.zeros((sequences, 1), jnp.float32),
    )
    combine = make_combine(fading_multiplier)
    arrived = prefix((end_numer, end_denom, length, cut), "seq", combine, identity, False)
    positions = jnp.arange(block_len, dtype=jnp.float32)
    alive = 1.0 - lax.cummax(flags, axis=1)
    rising = jnp.exp(-positions[:, None] * fading_multiplier[None, :])
    running_dividend = local_numer + alive[..., None] * rising[None] * arrived[0][:, None, :]
    running_divisor = local_denom + alive[..., None] * rising[None] * arrived[1][:, None, :]
    accumulated_sum = running_divisor + reward_scaled_pairs
    recurrent_average = (
        running_dividend + reward_scaled_pairs * payload_table_lines
    ) / accumulated_sum
    gate_sig = jax.nn.sigmoid(gate_rows)
    mixed = (gate_sig * recurrent_average).astype(jnp.bfloat16)
    first = inputs + product(mixed, full_output)
    normed_b, unit_b, factor_b = layer_norm(first, gain_second, bias_second)
    arriving_b = from_behind(normed_b[:, -1:, :], "seq", 1)
    before_b = attach_previous(normed_b, arriving_b, persisting_indicator)
    spread_b = normed_b - before_b
    expand_in = (before_b + spread_b * ratio_expand).astype(jnp.bfloat16)
    select_in = (before_b + spread_b * ratio_select).astype(jnp.bfloat16)
    expanded = product(expand_in, full_expand)
    selected = product(select_in, full_select)
    positive = jax.nn.relu(expanded)
    squared = (positive * positive).astype(jnp.bfloat16)
    contracted = product(squared, full_contract)
    select_sig = jax.nn.sigmoid(selected)
    block_out = (first + select_sig * contracted).astype(jnp.bfloat16)
    again = (
        lax.all_gather(mixing_lookup_projection, ("seq", "batch"), axis=0, tiled=True),
        lax.all_gather(mixing_payload_projection, ("seq", "batch"), axis=0, tiled=True),
        lax.all_gather(mixing_acceptor_projection, ("seq", "batch"), axis=0, tiled=True),
        lax.all_gather(mixing_result_projection, ("seq", "batch"), axis=0, tiled=True),
        lax.all_gather(feedforward_lookup_projection, ("seq", "batch"), axis=0, tiled=True),
        lax.all_gather(feedforward_acceptor_projection, ("seq", "batch"), axis=0, tiled=True),
        lax.all_gather(feedforward_payload_projection, ("seq", "batch"), axis=0, tiled=True),
    )
    full_key, full_value, full_gate, full_output, full_expand, full_select, full_contract = again
    upstream = upstream_adjoint.astype(jnp.float32)
    grad_contracted = (upstream * select_sig).astype(jnp.bfloat16)
    grad_selected = (upstream * contracted * select_sig * (1.0 - select_sig)).astype(jnp.bfloat16)
    grad_squared = product_back(grad_contracted, full_contract)
    grad_expanded = (2.0 * positive * grad_squared).astype(jnp.bfloat16)
    contract_grad = jnp.einsum(
        "scf,scd->fd", squared, grad_contracted, preferred_element_type=jnp.float32
    )
    expand_grad = outer_sum(expand_in, grad_expanded)
    select_grad = outer_sum(select_in, grad_selected)
    grad_expand_in = product_back(grad_expanded, full_expand)
    grad_select_in = product_back(grad_selected, full_select)
    expand_ratio_grad = jnp.sum(grad_expand_in * spread_b, axis=(0, 1))
    select_ratio_grad = jnp.sum(grad_select_in * spread_b, axis=(0, 1))
    grad_before_b = (
        grad_expand_in * (1.0 - ratio_expand) + grad_select_in * (1.0 - ratio_select)
    ) * persisting_indicator[..., None]
    arriving_gb = from_behind(grad_before_b[:, :1, :], "seq", -1)
    grad_normed_b = (
        grad_expand_in * ratio_expand
        + grad_select_in * ratio_select
        + attach_next(grad_before_b, arriving_gb)
    )
    grad_from_b, chan_gain_grad, chan_bias_grad = norm_back(
        grad_normed_b, unit_b, factor_b, gain_second
    )
    grad_first = upstream + grad_from_b
    grad_attended = grad_first.astype(jnp.bfloat16)
    output_grad = outer_sum(mixed, grad_attended)
    grad_mixed = product_back(grad_attended, full_output)
    grad_gates = (grad_mixed * recurrent_average * gate_sig * (1.0 - gate_sig)).astype(jnp.bfloat16)
    grad_wkv = grad_mixed * gate_sig
    adjoint_dividend = grad_wkv / accumulated_sum
    grad_denom = -grad_wkv * recurrent_average / accumulated_sum
    following_dividend, next_denom, lead_numer, lead_denom = reverse_sweep(
        adjoint_dividend, grad_denom, persisting_indicator, shrink
    )
    behind = prefix((lead_numer, lead_denom, length, cut), "seq", combine, identity, True)
    after = jnp.concatenate([flags[:, 1:], jnp.zeros_like(flags[:, :1])], axis=1)
    later_alive = 1.0 - lax.cummax(after, axis=1, reverse=True)
    falling = jnp.exp(-(block_len - 1.0 - positions)[:, None] * fading_multiplier[None, :])
    following_dividend = (
        following_dividend + later_alive[..., None] * falling[None] * behind[0][:, None, :]
    )
    next_denom = next_denom + later_alive[..., None] * falling[None] * behind[1][:, None, :]
    immediate_term = adjoint_dividend * payload_table_lines + grad_denom
    grad_keys = (
        exponentiated_lookup * (following_dividend * payload_table_lines + next_denom)
        + reward_scaled_pairs * immediate_term
    ).astype(jnp.bfloat16)
    adjoint_payloads = (
        exponentiated_lookup * following_dividend + reward_scaled_pairs * adjoint_dividend
    ).astype(jnp.bfloat16)
    present_reward_adjoint = jnp.sum(reward_scaled_pairs * immediate_term, axis=(0, 1))
    decay_grad = -shrink * jnp.sum(
        following_dividend * running_dividend + next_denom * running_divisor, axis=(0, 1)
    )
    key_grad = outer_sum(key_in, grad_keys)
    value_grad = outer_sum(value_in, adjoint_payloads)
    gate_grad = outer_sum(gate_in, grad_gates)
    grad_key_in = product_back(grad_keys, full_key)
    grad_value_in = product_back(adjoint_payloads, full_value)
    grad_gate_in = product_back(grad_gates, full_gate)
    key_ratio_grad = jnp.sum(grad_key_in * spread_a, axis=(0, 1))
    value_ratio_grad = jnp.sum(grad_value_in * spread_a, axis=(0, 1))
    gate_ratio_grad = jnp.sum(grad_gate_in * spread_a, axis=(0, 1))
    grad_before_a = (
        grad_key_in * (1.0 - ratio_key)
        + grad_value_in * (1.0 - ratio_value)
        + grad_gate_in * (1.0 - ratio_gate)
    ) * persisting_indicator[..., None]
    arriving_ga = from_behind(grad_before_a[:, :1, :], "seq", -1)
    grad_normed_a = (
        grad_key_in * ratio_key
        + grad_value_in * ratio_value
        + grad_gate_in * ratio_gate
        + attach_next(grad_before_a, arriving_ga)
    )
    grad_from_a, attn_gain_grad, attn_bias_grad = norm_back(
        grad_normed_a, unit_a, factor_a, gain_first
    )
    tokens_grad = grad_first + grad_from_a
    shares = (
        lax.psum_scatter(key_grad, ("seq", "batch"), scatter_dimension=0, tiled=True),
        lax.psum_scatter(value_grad, ("seq", "batch"), scatter_dimension=0, tiled=True),
        lax.psum_scatter(gate_grad, ("seq", "batch"), scatter_dimension=0, tiled=True),
        lax.psum_scatter(output_grad, ("seq", "batch"), scatter_dimension=0, tiled=True),
        lax.psum_scatter(expand_grad, ("seq", "batch"), scatter_dimension=0, tiled=True),
        lax.psum_scatter(select_grad, ("seq", "batch"), scatter_dimension=0, tiled=True),
        lax.psum_scatter(contract_grad, ("seq", "batch"), scatter_dimension=0, tiled=True),
        lax.psum_scatter(attn_gain_grad, ("seq", "batch"), scatter_dimension=0, tiled=True),
        lax.psum_scatter(attn_bias_grad, ("seq", "batch"), scatter_dimension=0, tiled=True),
        lax.psum_scatter(chan_gain_grad, ("seq", "batch"), scatter_dimension=0, tiled=True),
        lax.psum_scatter(chan_bias_grad, ("seq", "batch"), scatter_dimension=0, tiled=True),
        lax.psum_scatter(key_ratio_grad, ("seq", "batch"), scatter_dimension=0, tiled=True),
        lax.psum_scatter(value_ratio_grad, ("seq", "batch"), scatter_dimension=0, tiled=True),
        lax.psum_scatter(gate_ratio_grad, ("seq", "batch"), scatter_dimension=0, tiled=True),
        lax.psum_scatter(expand_ratio_grad, ("seq", "batch"), scatter_dimension=0, tiled=True),
        lax.psum_scatter(select_ratio_grad, ("seq", "batch"), scatter_dimension=0, tiled=True),
        lax.psum_scatter(decay_grad, ("seq", "batch"), scatter_dimension=0, tiled=True),
        lax.psum_scatter(present_reward_adjoint, ("seq", "batch"), scatter_dimension=0, tiled=True),
    )
    return (
        block_out,
        tokens_grad,
        shares[0],
        shares[1],
        shares[2],
        shares[3],
        shares[4],
        shares[5],
        shares[6],
        shares[7],
        shares[8],
        shares[9],
        shares[10],
        shares[11],
        shares[12],
        shares[13],
        shares[14],
        shares[15],
        shares[16],
        shares[17],
    )


def solution(mesh):
    return jax.shard_map(
        body,
        mesh=mesh,
        in_specs=(
            P("batch", "seq", None),
            P("batch", "seq"),
            P(("seq", "batch"), None),
            P(("seq", "batch"), None),
            P(("seq", "batch"), None),
            P(("seq", "batch"), None),
            P(("seq", "batch"), None),
            P(("seq", "batch"), None),
            P(("seq", "batch"), None),
            P(("seq", "batch")),
            P(("seq", "batch")),
            P(("seq", "batch")),
            P(("seq", "batch")),
            P(("seq", "batch")),
            P(("seq", "batch")),
            P(("seq", "batch")),
            P(("seq", "batch")),
            P(("seq", "batch")),
            P(("seq", "batch")),
            P(("seq", "batch")),
            P("batch", "seq", None),
        ),
        out_specs=(
            P("batch", "seq", None),
            P("batch", "seq", None),
            P(("seq", "batch"), None),
            P(("seq", "batch"), None),
            P(("seq", "batch"), None),
            P(("seq", "batch"), None),
            P(("seq", "batch"), None),
            P(("seq", "batch"), None),
            P(("seq", "batch"), None),
            P(("seq", "batch")),
            P(("seq", "batch")),
            P(("seq", "batch")),
            P(("seq", "batch")),
            P(("seq", "batch")),
            P(("seq", "batch")),
            P(("seq", "batch")),
            P(("seq", "batch")),
            P(("seq", "batch")),
            P(("seq", "batch")),
            P(("seq", "batch")),
        ),
        check_vma=False,
    )
```

profile of v0, /device:TPU:0, one launch (start us, length us, event | category | flops | bytes accessed | tf_op | source)
XLA Modules:
  0.0 1936.6 jit_solution(11658735622619614273)
XLA Ops:
  20.4 42.3 %all-reduce.95 = (bf16[768]{0:T(1024)(128)(2,1)S(1)}, bf16[768]{0:T(1024)(128)(2,1)S(1)}, bf16[768]{0:T(1024)(128)(2,1)S(1)}, bf16[768]{0:T(1024)(128)(2,1)S(1)}...) all-reduce(bf16[768]{0:T(1024)(128)(2,1)S(1)} %dynamic-update-slice, ...), channel_id=1, replica_groups=mesh['seq'=8,'batch'=4] {'seq','batch'}, use_global_device_ids=true, to_apply=%add.71 | all-reduce | flops 8448 | bytes 33792
  75.0 16.5 all-reduce.94
  107.8 9.7 slice.696
  140.4 9.8 slice.759
  311.4 9.7 slice.752
  435.5 13.9 all-gather
  483.9 13.9 all-gather.2
  558.3 12.8 slice.803
  571.2 12.8 slice.809
  584.0 12.8 slice.802
  603.3 10.0 fusion.13
  613.3 10.6 fusion.9
  631.4 10.9 multiply_convert_fusion
  733.9 12.8 slice.807
  746.7 12.8 slice.805
  759.5 12.8 slice.873
  772.3 12.8 slice.871
  930.8 12.9 slice.862
  943.7 12.9 slice.908
  1078.7 25.3 %slice.911 = f32[4,255,768]{2,1,0:T(8,128)} reverse(f32[4,255,768]{2,1,0:T(8,128)} %slice_add_fusion.12), dimensions={1} | reverse | bytes 6266880 | tf_op jit(solution)/shard_map/slice | solution.py:118
  1123.1 25.2 %slice.864 = f32[4,255,768]{2,1,0:T(8,128)} reverse(f32[4,255,768]{2,1,0:T(8,128)} %slice_add_fusion), dimensions={1} | reverse | bytes 6266880 | tf_op jit(solution)/shard_map/slice | solution.py:117
  1154.9 27.6 %all-gather.3 = f32[32,1,768]{2,1,0:T(1,128)S(1)} all-gather(f32[4,1,768]{2,1,0:T(1,128)S(1)} %slice.1179), channel_id=5, replica_groups=mesh['seq'=8,'batch'=4] {'seq'}, dimensions={0}, use_global_device_ids=true | all-gather | bytes 110592 | tf_op jit(solution)/shard_map/all_gather | solution.py:19
  1189.4 13.9 all-gather.4
  1204.3 18.8 while.33
  1253.9 10.0 convolution_bitcast_fusion.1
  1265.3 11.5 convolution_bitcast_fusion
  1294.0 40.5 %all-reduce.93 = (f32[768]{0:T(1024)S(1)}, f32[768]{0:T(1024)S(1)}, f32[768]{0:T(1024)S(1)}, f32[768]{0:T(1024)S(1)}, f32[768]{0:T(1024)S(1)}, /*index=5*/f32[76...) all-reduce(f32[768]{0:T(1024)S(1)} %get-tuple-element.307, ...), channel_id=14, replica_groups=mesh['seq'=8,'batch'=4] {'seq','batch'}, use_global_device_ids=true, to_apply=%region_25.26.clone | all-reduce | flops 8448 | bytes 67584
  1345.5 92.7 %reduce-scatter.10.cloned.1.call-done = f32[24,768]{1,0:T(8,128)} async-done(((f32[768,768]{1,0:T(8,128)}), f32[24,768]{1,0:T(8,128)}) %reduce-scatter.10.cloned.1.call-update) | async-done | bytes 73744 | tf_op jit(solution)/shard_map/reduce_scatter | solution.py:334
  1438.2 104.7 %reduce-scatter.12.cloned.1.call-done = f32[24,768]{1,0:T(8,128)} async-done(((f32[768,768]{1,0:T(8,128)}), f32[24,768]{1,0:T(8,128)}) %reduce-scatter.12.cloned.1.call-update) | async-done | bytes 73744 | tf_op jit(solution)/shard_map/reduce_scatter | solution.py:335
  1542.9 103.8 %reduce-scatter.14.cloned.1.call-done = f32[24,768]{1,0:T(8,128)} async-done(((f32[768,768]{1,0:T(8,128)}), f32[24,768]{1,0:T(8,128)}) %reduce-scatter.14.cloned.1.call-update) | async-done | bytes 73744 | tf_op jit(solution)/shard_map/reduce_scatter | solution.py:336
  1646.7 141.9 %reduce-scatter.16.cloned.1.call-done = f32[24,3072]{1,0:T(8,128)} async-done(((f32[768,3072]{1,0:T(8,128)}), f32[24,3072]{1,0:T(8,128)}) %reduce-scatter.16.cloned.1.call-update) | async-done | bytes 294928 | tf_op jit(solution)/shard_map/reduce_scatter | solution.py:337
  1788.6 141.1 %reduce-scatter.20.cloned.1.call-done = f32[96,768]{1,0:T(8,128)} async-done(((f32[3072,768]{1,0:T(8,128)}), f32[96,768]{1,0:T(8,128)}) %reduce-scatter.20.cloned.1.call-update) | async-done | bytes 294928 | tf_op jit(solution)/shard_map/reduce_scatter | solution.py:339
  (761 shorter events, 918.8 us)
Async XLA Ops:
  7.2 57.3 %copy-start = (bf16[4,256,768]{2,1,0:T(8,128)(2,1)S(1)}, bf16[4,256,768]{2,1,0:T(8,128)(2,1)}, u32[]{:S(2)}) copy-start(bf16[4,256,768]{2,1,0:T(8,128)(2,1)} %param.25) | copy-start | bytes 4718596
  7.2 121.5 %all-gather.17.cloned.1.call-start = ((), (), s32[]{:S(2)}) async-start(), calls=%async_computation.9 | async-start | bytes 1216512 | tf_op jit(solution)/shard_map/all_gather | solution.py:147
  7.9 125.6 %all-gather.15.cloned.1.call-start = ((), (), s32[]{:S(2)}) async-start(), calls=%async_computation.8 | async-start | bytes 1216512 | tf_op jit(solution)/shard_map/all_gather | solution.py:146
  8.7 519.1 %all-gather.13.cloned.1.call-start = ((), (), s32[]{:S(2)}) async-start(), calls=%async_computation.7 | async-start | bytes 1216512 | tf_op jit(solution)/shard_map/all_gather | solution.py:148
  9.4 527.0 %all-gather.19.cloned.1.call-start = ((), (), s32[]{:S(2)}) async-start(), calls=%async_computation.10 | async-start | bytes 1216512 | tf_op jit(solution)/shard_map/all_gather | solution.py:149
  10.0 593.3 %all-gather.23.cloned.1.call-start = ((), (), s32[]{:S(2)}) async-start(), calls=%async_computation.12 | async-start | bytes 4866048 | tf_op jit(solution)/shard_map/all_gather | solution.py:150
  10.6 602.7 %all-gather.25.cloned.1.call-start = ((), (), s32[]{:S(2)}) async-start(), calls=%async_computation.13 | async-start | bytes 4866048 | tf_op jit(solution)/shard_map/all_gather | solution.py:152
  11.2 612.7 %all-gather.21.cloned.1.call-start = ((), (), s32[]{:S(2)}) async-start(), calls=%async_computation.11 | async-start | bytes 1216512 | tf_op jit(solution)/shard_map/all_gather | solution.py:151
  62.8 28.9 %copy-start.118 = (bf16[768]{0:T(1024)(128)(2,1)}, bf16[768]{0:T(1024)(128)(2,1)S(1)}, u32[]{:S(2)}) copy-start(bf16[768]{0:T(1024)(128)(2,1)S(1)} %get-tuple-element.368) | copy-start | bytes 4612
  62.8 39.3 %copy-start.68 = (f32[768]{0:T(1024)}, f32[768]{0:T(1024)S(1)}, u32[]{:S(2)}) copy-start(f32[768]{0:T(1024)S(1)} %convert_element_type.89) | copy-start | bytes 9220
  62.8 39.2 %copy-start.59 = (f32[768]{0:T(1024)}, f32[768]{0:T(1024)S(1)}, u32[]{:S(2)}) copy-start(f32[768]{0:T(1024)S(1)} %convert_element_type.88) | copy-start | bytes 9220
  64.5 37.5 %copy-start.57 = (f32[4,256]{1,0:T(4,128)}, f32[4,256]{1,0:T(4,128)S(1)}, u32[]{:S(2)}) copy-start(f32[4,256]{1,0:T(4,128)S(1)} %broadcast_multiply_fusion.8) | copy-start | bytes 12292
  65.2 36.9 %copy-start.61 = (f32[4,256]{1,0:T(4,128)}, f32[4,256]{1,0:T(4,128)S(1)}, u32[]{:S(2)}) copy-start(f32[4,256]{1,0:T(4,128)S(1)} %add_rsqrt_fusion.1) | copy-start | bytes 12292
  67.5 34.6 %collective-permute-start = (f32[4,1,768]{2,1,0:T(1,128)S(1)}, f32[4,1,768]{2,1,0:T(1,128)S(1)}, u32[]{:S(2)}, u32[]{:S(2)}) collective-permute-start(f32[4,1,768]{2,1,0:T(1,128)S(1)} %slice.914), channel_id=1, source_target_pairs={{0,4},{4,8},{8,12},{12,16},{16,20},{20,24},{24,28},{1,5},{5,9},{9,... | collective-permute-start | bytes 36872 | tf_op jit(solution)/shard_map/ppermute | solution.py:12
  68.9 1276.6 %reduce-scatter.18.cloned.1.call-start = ((), (), s32[]{:S(2)}) async-start(), calls=%async_computation.19 | async-start | bytes 2433024 | tf_op jit(solution)/shard_map/reduce_scatter | solution.py:338
  69.0 38.7 %copy-start.52 = (f32[4,256]{1,0:T(4,128)}, f32[4,256]{1,0:T(4,128)S(1)}, u32[]{:S(2)}) copy-start(f32[4,256]{1,0:T(4,128)S(1)} %get-tuple-element.486) | copy-start | bytes 12292
  140.4 387.4 %copy-start.4 = (f32[4,256,768]{2,1,0:T(8,128)}, f32[4,256,768]{2,1,0:T(8,128)S(1)}, u32[]{:S(2)}) copy-start(f32[4,256,768]{2,1,0:T(8,128)S(1)} %get-tuple-element.488) | copy-start | bytes 9437188
  498.2 29.7 %copy-start.48 = (f32[4,768]{1,0:T(4,128)}, f32[4,768]{1,0:T(4,128)S(1)}, u32[]{:S(2)}) copy-start(f32[4,768]{1,0:T(4,128)S(1)} %get-tuple-element.242) | copy-start | bytes 36868
  543.1 53.8 %collective-permute-start.1 = (f32[4,1,768]{2,1,0:T(1,128)S(1)}, f32[4,1,768]{2,1,0:T(1,128)S(1)}, u32[]{:S(2)}, u32[]{:S(2)}) collective-permute-start(f32[4,1,768]{2,1,0:T(1,128)S(1)} %slice.972), channel_id=1, source_target_pairs={{0,4},{4,8},{8,12},{12,16},{16,20},{20,24},{24,28},{1,5},{5,9},{9,... | collective-permute-start | bytes 36872 | tf_op jit(solution)/shard_map/ppermute | solution.py:12
  655.9 8.1 collective-permute-start.2
  663.9 681.6 %reduce-scatter.8.cloned.1.call-start = ((), (), s32[]{:S(2)}) async-start(), calls=%async_computation.14 | async-start | bytes 2433024 | tf_op jit(solution)/shard_map/reduce_scatter | solution.py:333
  1154.0 50.3 %copy-start.51 = (f32[768]{0:T(1024)S(1)}, f32[768]{0:T(1024)}, u32[]{:S(2)}) copy-start(f32[768]{0:T(1024)} %copy-done.50) | copy-start | bytes 9220
  1154.0 50.3 %copy-start.126 = (f32[8,1]{0,1:T(1,128)S(1)}, f32[8,1]{0,1:T(1,128)}, u32[]{:S(2)}) copy-start(f32[8,1]{0,1:T(1,128)} %get-tuple-element.777) | copy-start | bytes 100
  1182.7 40.5 %copy-start.49 = (f32[4,768]{1,0:T(4,128)S(1)}, f32[4,768]{1,0:T(4,128)}, u32[]{:S(2)}) copy-start(f32[4,768]{1,0:T(4,128)} %copy-done.48) | copy-start | bytes 36868
  1182.7 40.5 %copy-start.98 = (f32[1,4,2,128]{3,1,2,0:T(4,128)S(1)}, f32[1,4,2,128]{3,1,2,0:T(4,128)}, u32[]{:S(2)}) copy-start(f32[1,4,2,128]{3,1,2,0:T(4,128)} %copy.96) | copy-start | bytes 12292
  1182.7 40.5 %copy-start.99 = (f32[1,4,2,128]{3,1,2,0:T(4,128)S(1)}, f32[1,4,2,128]{3,1,2,0:T(4,128)}, u32[]{:S(2)}) copy-start(f32[1,4,2,128]{3,1,2,0:T(4,128)} %copy.95) | copy-start | bytes 12292
  1236.3 201.9 %reduce-scatter.10.cloned.1.call-start = ((), (), s32[]{:S(2)}) async-start(), calls=%async_computation.15 | async-start | bytes 2433024 | tf_op jit(solution)/shard_map/reduce_scatter | solution.py:334
  1244.2 298.7 %reduce-scatter.12.cloned.1.call-start = ((), (), s32[]{:S(2)}) async-start(), calls=%async_computation.16 | async-start | bytes 2433024 | tf_op jit(solution)/shard_map/reduce_scatter | solution.py:335
  1249.5 397.2 %reduce-scatter.14.cloned.1.call-start = ((), (), s32[]{:S(2)}) async-start(), calls=%async_computation.17 | async-start | bytes 2433024 | tf_op jit(solution)/shard_map/reduce_scatter | solution.py:336
  1253.9 534.8 %reduce-scatter.16.cloned.1.call-start = ((), (), s32[]{:S(2)}) async-start(), calls=%async_computation.18 | async-start | bytes 9732096 | tf_op jit(solution)/shard_map/reduce_scatter | solution.py:337
  1263.9 665.9 %reduce-scatter.20.cloned.1.call-start = ((), (), s32[]{:S(2)}) async-start(), calls=%async_computation.20 | async-start | bytes 9732096 | tf_op jit(solution)/shard_map/reduce_scatter | solution.py:339
  1284.6 3.1 collective-permute-start.3
  (116 other events, 931.5 us)
Sparse Core Ops, SparseCore 0:
  10.9 56.8 all-gather.16
  70.7 52.9 all-gather.14
  126.6 52.9 all-gather.12
  182.4 52.9 all-gather.18
  238.1 62.4 all-gather.22
  303.4 62.3 all-gather.24
  368.7 52.8 all-gather.20
  664.1 114.0 reduce-scatter.17
  1236.4 97.8 reduce-scatter.7
  1340.0 98.1 reduce-scatter.9
  1444.9 97.9 reduce-scatter.11
  1548.6 98.0 reduce-scatter.13
  1654.2 134.4 reduce-scatter.15
  1795.0 134.7 reduce-scatter.19
where the time goes:
time: 1970 us; the launch traced here: 1940 us
  local copies, waits for them, and re-layouts  775 us (39%)
  waiting for transfers between devices  589 us (30%)
  other arithmetic  255 us (13%)
  blocking collectives  169 us (9%)
  matrix products  122 us (6%)
    slice x79, local copies, waits for them, and re-layouts, reverse_sweep(): lax.associative_scan(affine_compose, (keep_now * shrink, keep_now * adjoi...  296 us
    slice x72, local copies, waits for them, and re-layouts, forward_sweep(): lax.associative_scan(affine_compose, (multiplier, exponentiated_lookup *...  191 us
    reduce_scatter x1, waiting for transfers between devices, body(): lax.psum_scatter(expand_grad, ('seq', 'batch'), scatter_dimension=0, tile...  142 us
    reduce_scatter x1, waiting for transfers between devices, body(): lax.psum_scatter(contract_grad, ('seq', 'batch'), scatter_dimension=0, ti...  141 us
    reduce_scatter x1, waiting for transfers between devices, body(): lax.psum_scatter(gate_grad, ('seq', 'batch'), scatter_dimension=0, tiled=...  105 us
    reduce_scatter x1, waiting for transfers between devices, body(): lax.psum_scatter(output_grad, ('seq', 'batch'), scatter_dimension=0, tile...  104 us
    unnamed x3, blocking collectives  99.4 us
    reduce_scatter x1, waiting for transfers between devices, body(): lax.psum_scatter(value_grad, ('seq', 'batch'), scatter_dimension=0, tiled...  92.7 us
  transfers between devices with their start and end apart: 18, of which 6 were waited for; matrix products, arithmetic and copies ran while one was open for 57% of the time, Pallas kernels for 0%

commit v1 on v0

--- a/solution.py
+++ b/solution.py
@@ -1,9 +1,1119 @@
 import jax
 import jax.numpy as jnp
 from jax import lax
+from jax.experimental import pallas as pl
+from jax.experimental.pallas import tpu as pltpu
 from jax.sharding import PartitionSpec as P
 
+BOTH = ("seq", "batch")
+MESH = pl.DeviceIdType.MESH
+BF = jnp.bfloat16
+F32 = jnp.float32
+WIDE = 768
+ROWS_MAIN = 224
+ROWS_LAST = 96
+GATHER_CHUNKS = ((0, 0, 80, 48), (0, 80, 48, 16), (0, 128, 48, 32), (0, 176, 48, 16), (1, 0, 48, 32), (1, 48, 48, 16))
+SCATTER_CHUNKS = ((1, 0, 48, 32), (1, 48, 48, 16), (0, 128, 48, 32), (0, 176, 48, 16), (0, 80, 48, 16), (0, 0, 80, 48))
+COUNT = len(GATHER_CHUNKS)
+
+
+class Place:
+    def __init__(self):
+        self.s = lax.axis_index("seq")
+        self.b = lax.axis_index("batch")
+        self.z, self.c = self.s // 2, self.s % 2
+        y, x = self.b // 2, self.b % 2
+        self.bx, self.by, self.bd = y * 2 + 1 - x, (1 - y) * 2 + x, (1 - y) * 2 + 1 - x
+        self.depth = lax.axis_size("seq") // 2
+        self.x, self.y = (self.s, self.bx), (self.s, self.by)
+        self.core = (self.z * 2 + 1 - self.c, self.b)
+
+    def along(self, step):
+        z = lax.rem(self.z + step, self.depth)
+        return z, (z * 2 + self.c, self.b)
+
+    def back(self, step):
+        return lax.rem(self.z + self.depth - step, self.depth)
+
+
+def rdma(src, dst, sems, send, recv, to):
+    return pltpu.make_async_remote_copy(
+        src_ref=src, dst_ref=dst, send_sem=sems.at[send], recv_sem=sems.at[recv], device_id=to, device_id_type=MESH
+    )
+
+
+def enter(place):
+    barrier = pltpu.get_barrier_semaphore()
+    count = 0
+    peers = [place.x, place.y, place.core] + [place.along(d)[1] for d in range(1, place.depth)]
+    for peer in peers:
+        pl.semaphore_signal(barrier, inc=1, device_id=peer, device_id_type=MESH)
+    pl.semaphore_wait(barrier, len(peers))
+
+
+class Gather:
+    def __init__(self, place, arrays, sems):
+        self.p, self.arrays, self.sems = place, arrays, sems
+
+    def copies(self, k):
+        p, sems = self.p, self.sems.at[k]
+        a, r0, n, nx = GATHER_CHUNKS[k]
+        ref = self.arrays[a]
+        whole, part_x, part_y = pl.ds(r0, n), pl.ds(r0, nx), pl.ds(r0 + nx, n - nx)
+        own = ref.at[p.z, p.c, p.b, whole]
+        col = lambda c, b, rows: ref.at[:, c, b, rows]
+        out = {}
+        for d in range(1, p.depth):
+            out["z", d] = rdma(own, own, sems, 2 * d - 2, 2 * d - 1, p.along(d)[1])
+        out["x"] = rdma(col(p.c, p.b, whole), col(p.c, p.b, whole), sems, 6, 7, p.x)
+        out["y"] = rdma(col(p.c, p.b, whole), col(p.c, p.b, whole), sems, 8, 9, p.y)
+        out["dx"] = rdma(col(p.c, p.by, part_x), col(p.c, p.by, part_x), sems, 10, 11, p.x)
+        out["dy"] = rdma(col(p.c, p.bx, part_y), col(p.c, p.bx, part_y), sems, 12, 13, p.y)
+        for j, b in enumerate((p.b, p.bx, p.by)):
+            pass
+        out["c", 0] = rdma(col(p.c, p.b, whole), col(p.c, p.b, whole), sems, 14, 15, p.core)
+        out["c", 1] = rdma(col(p.c, p.bx, whole), col(p.c, p.bx, whole), sems, 16, 17, p.core)
+        out["c", 2] = rdma(col(p.c, p.by, whole), col(p.c, p.by, whole), sems, 18, 19, p.core)
+        out["c", 3] = rdma(col(p.c, p.bd, whole), col(p.c, p.bd, whole), sems, 20, 21, p.core)
+        return out
+
+    def arrivals(self, k):
+        p, sems = self.p, self.sems.at[k]
+        a, r0, n, nx = GATHER_CHUNKS[k]
+        ref = self.arrays[a]
+        whole, part_x, part_y = pl.ds(r0, n), pl.ds(r0, nx), pl.ds(r0 + nx, n - nx)
+        col = lambda c, b, rows: ref.at[:, c, b, rows]
+        at = lambda view, recv, to: rdma(view, view, sems, recv - 1, recv, to)
+        out = {}
+        for d in range(1, p.depth):
+            out["z", d] = at(ref.at[p.back(d), p.c, p.b, whole], 2 * d - 1, p.along(d)[1])
+        out["x"] = at(col(p.c, p.bx, whole), 7, p.x)
+        out["y"] = at(col(p.c, p.by, whole), 9, p.y)
+        out["dx"] = at(col(p.c, p.bd, part_x), 11, p.x)
+        out["dy"] = at(col(p.c, p.bd, part_y), 13, p.y)
+        for j, b in enumerate((p.b, p.bx, p.by, p.bd)):
+            out["c", j] = at(col(1 - p.c, b, whole), 15 + 2 * j, p.core)
+        return out
+
+    def stage(self, number, k):
+        if not 0 <= k < COUNT:
+            return
+        send, come = self.copies(k), self.arrivals(k)
+        if number == 0:
+            for d in range(1, self.p.depth):
+                send["z", d].start()
+        elif number == 1:
+            for d in range(1, self.p.depth):
+                come["z", d].wait_recv()
+            send["x"].start()
+            send["y"].start()
+            send["c", 0].start()
+        elif number == 2:
+            come["x"].wait_recv()
+            come["y"].wait_recv()
+            send["dx"].start()
+            send["dy"].start()
+            send["c", 1].start()
+            send["c", 2].start()
+        elif number == 3:
+            come["dx"].wait_recv()
+            come["dy"].wait_recv()
+            send["c", 3].start()
+        elif number == 4:
+            for j in range(4):
+                come["c", j].wait_recv()
+        elif number == 5:
+            for copy in send.values():
+                copy.wait_send()
+
+    def tick(self, t):
+        for number in range(5):
+            self.stage(number, t - number)
+
+
+class Scatter:
+    def __init__(self, place, packed, from_core, near, diag, line, out, sems, credits):
+        self.p, self.packed, self.from_core, self.near = place, packed, from_core, near
+        self.diag, self.line, self.out, self.sems, self.credits = diag, line, out, sems, credits
+
+    def stage(self, number, k):
+        p, sems = self.p, self.sems.at[k]
+        a, r0, n, nx = SCATTER_CHUNKS[k]
+        ref, slot, depth = self.packed[a], k % 2, p.depth
+        f0 = r0 if a == 0 else r0 + ROWS_MAIN
+        whole, part_x, part_y = pl.ds(r0, n), pl.ds(r0, nx), pl.ds(r0 + nx, n - nx)
+        core = lambda: rdma(ref.at[:, 1 - p.c, :, whole], self.from_core.at[slot, :, :, pl.ds(0, n)], sems, 0, 1, p.core)
+        diag_x = lambda: rdma(ref.at[:, p.c, p.bd, part_x], self.diag.at[slot, :, pl.ds(0, nx)], sems, 2, 3, p.x)
+        diag_y = lambda: rdma(ref.at[:, p.c, p.bd, part_y], self.diag.at[slot, :, pl.ds(nx, n - nx)], sems, 4, 5, p.y)
+        near_x = lambda: rdma(ref.at[:, p.c, p.bx, whole], self.near.at[slot, 0, :, pl.ds(0, n)], sems, 6, 7, p.x)
+        near_y = lambda: rdma(ref.at[:, p.c, p.by, whole], self.near.at[slot, 1, :, pl.ds(0, n)], sems, 8, 9, p.y)
+
+        def along(d):
+            z, to = p.along(d)
+            return rdma(ref.at[z, p.c, p.b, whole], self.line.at[d - 1, pl.ds(f0, n)], sems, 8 + 2 * d, 9 + 2 * d, to)
+
+        def ready(*which):
+            if k >= 2:
+                for w in which:
+                    pl.semaphore_wait(self.credits.at[w], 1)
+
+        def free(which, to):
+            if k + 2 < COUNT:
+                pl.semaphore_signal(self.credits.at[which], inc=1, device_id=to, device_id_type=MESH)
+
+        if number == 0:
+            ready(0)
+            core().start()
+        elif number == 1:
+            core().wait_recv()
+
+            @pl.loop(0, depth * 4)
+            def _(i):
+                z, b = i // 4, i % 4
+                ref[z, p.c, b, r0 : r0 + n] = (
+                    ref[z, p.c, b, r0 : r0 + n].astype(F32) + self.from_core[slot, z, b, 0:n].astype(F32)
+                ).astype(BF)
+
+            free(0, p.core)
+            ready(1, 2)
+            diag_x().start()
+            diag_y().start()
+        elif number == 2:
+            diag_x().wait_recv()
+            diag_y().wait_recv()
+
+            @pl.loop(0, depth)
+            def _(z):
+                for b, s0, m in ((p.by, 0, nx), (p.bx, nx, n - nx)):
+                    ref[z, p.c, b, r0 + s0 : r0 + s0 + m] = (
+                        ref[z, p.c, b, r0 + s0 : r0 + s0 + m].astype(F32) + self.diag[slot, z, s0 : s0 + m].astype(F32)
+                    ).astype(BF)
+
+            free(1, p.x)
+            free(2, p.y)
+            ready(3, 4)
+            near_x().start()
+            near_y().start()
+        elif number == 3:
+            near_x().wait_recv()
+            near_y().wait_recv()
+
+            @pl.loop(0, depth)
+            def _(z):
+                ref[z, p.c, p.b, r0 : r0 + n] = (
+                    ref[z, p.c, p.b, r0 : r0 + n].astype(F32)
+                    + self.near[slot, 0, z, 0:n].astype(F32)
+                    + self.near[slot, 1, z, 0:n].astype(F32)
+                ).astype(BF)
+
+            free(3, p.x)
+            free(4, p.y)
+            for d in range(1, depth):
+                along(d).start()
+        elif number == 4:
+            for d in range(1, depth):
+                along(d).wait_recv()
+            total = ref[p.z, p.c, p.b, r0 : r0 + n].astype(F32)
+            for d in range(1, depth):
+                total = total + self.line[d - 1, f0 : f0 + n].astype(F32)
+            self.out[f0 : f0 + n] = total
+        elif number == 5:
+            for each in (core, diag_x, diag_y, near_x, near_y):
+                each().wait_send()
+            for d in range(1, depth):
+                along(d).wait_send()
+
+
 EPSILON = 1e-05
+TOK = 1024
+SEQS = 4
+SPAN = 256
+STEPS = 32
+SEG = 8
+LANE = 128
+WINDOW = 256
+VECTORS = 11
+
+
+def window_of(i):
+    return min(i * 24 // LANE, WIDE // LANE - 2) * LANE
+
+
+def spread_lanes(v):
+    return jnp.concatenate([v] * (WIDE // LANE), axis=1)
+
+
+def unit_norm(v):
+    center = v - jnp.mean(v, axis=-1, keepdims=True)
+    factor = lax.rsqrt(jnp.mean(center * center, axis=-1, keepdims=True) + EPSILON)
+    return center * factor, factor
+
+
+def sigmoid(v):
+    return 1.0 / (1.0 + jnp.exp(-v))
+
+
+def first_rows(halo_row, last_group):
+    moved = pltpu.roll(last_group, 1, axis=0)
+    at_top = lax.broadcasted_iota(jnp.int32, moved.shape, 0) == 0
+    return jnp.where(at_top, halo_row, moved)
+
+
+def permute_in(src, dst, tmp):
+    @pl.loop(0, SEQS)
+    def _(j):
+        base = pl.multiple_of(j * SPAN, SPAN)
+        for l in range(WIDE // LANE):
+            tmp[l] = src[pl.ds(base, SPAN), l * LANE : (l + 1) * LANE].astype(F32)
+
+        @pl.loop(0, STEPS // 2)
+        def _(s):
+            for l in range(WIDE // LANE):
+                two = jnp.concatenate([tmp[l, pl.ds(2 * s, SEG, stride=STEPS), :], tmp[l, pl.ds(2 * s + 1, SEG, stride=STEPS), :]], axis=0)
+                dst[pl.ds(pl.multiple_of(base + s * 16, 16), 16), l * LANE : (l + 1) * LANE] = two.astype(BF)
+
+
+class Spill:
+    def __init__(self, sems):
+        self.sems, self.copies, self.used = sems, {}, 0
+
+    def start(self, name, src, dst):
+        self.copies[name] = pltpu.make_async_copy(src, dst, self.sems.at[self.used])
+        self.used += 1
+        self.copies[name].start()
+
+    def wait(self, *names):
+        for name in names or list(self.copies):
+            self.copies.pop(name).wait()
+
+
+class Line:
+    def __init__(self, place):
+        self.p = place
+        self.n = lax.axis_size("seq")
+
+    def all(self, buf, sems):
+        p, copies = self.p, []
+        for d in range(1, self.n):
+            to = (lax.rem(p.s + d, self.n), p.b)
+            copies.append(rdma(buf.at[p.s], buf.at[p.s], sems, d, self.n + d, to))
+        return copies
+
+    def shift(self, src, dst, sems, step):
+        return rdma(src, dst, sems, 0, 1, (lax.rem(self.p.s + self.n + step, self.n), self.p.b))
+
+
+def relayout(st, dst, depth, r0, n, targets):
+    @pl.loop(0, depth * 2)
+    def _(i):
+        z, c = i // 2, i % 2
+        slabs = [st[z, c, b, r0 : r0 + n].astype(F32) for b in range(4)]
+        rows = pl.ds(pl.multiple_of(i * 96, 96), 96)
+        for index, at in targets:
+            dst[index, rows] = jnp.concatenate([v[at : at + 24] for v in slabs], axis=0).astype(BF)
+
+
+def matmul(left, right, out, rows=512):
+    @pl.loop(0, TOK // rows)
+    def _(i):
+        r = pl.ds(pl.multiple_of(i * rows, rows), rows)
+        out[r] = jnp.dot(left[r], right[...], preferred_element_type=F32)
+
+
+def forward_kernel(x_in, keep_in, up_in, vec_in, wk, wv, wr, wo, ws, we_in, wc_in,
+                   o_w, o_e, o_c, o_ki, o_spa, o_spb, o_mixed, o_ei, o_si, o_gc, o_gs, o_xp, o_up, o_sq, o_pkc,
+                   o_kvg, o_nd, o_first, o_vec, o_alive, o_bo,
+                   st, cw, wd, we, u0, xp, u1, gyp, tmp, keep, xa, ki, kvg, nd, spb, vb, vec, states, alive, seg, carry, hx, hx_got, hb, hb_got,
+                   gsems, vsems, asems, ssems, hsems, lsems):
+    place = Place()
+    line = Line(place)
+    depth = place.depth
+    devices = depth * 8
+    me = place.s * 4 + place.b
+    spill = Spill(lsems)
+    spill.start("x", x_in, u0)
+    spill.start("keep", keep_in, keep)
+    spill.start("up", up_in, u1)
+    barrier = pltpu.get_barrier_semaphore()
+    for d in range(1, devices):
+        other = lax.rem(me + d, devices)
+        pl.semaphore_signal(barrier, inc=1, device_id=(other // 4, other % 4), device_id_type=MESH)
+    z, c, b = place.z, place.c, place.b
+    as32 = lambda ref: ref[...].astype(F32)
+    join = lambda *v: jnp.concatenate(v, axis=0).astype(BF)
+    st[z, c, b, 0:48] = join(as32(wk), as32(wv))
+    st[z, c, b, 48:80] = join(as32(wr), jnp.zeros((8, WIDE), F32))
+    st[z, c, b, 80:128] = join(as32(wo), as32(ws))
+    e = as32(we_in)
+    for h in range(2):
+        st[z, c, b, 128 + 48 * h : 176 + 48 * h] = join(e[:, 2 * h * WIDE : (2 * h + 1) * WIDE], e[:, (2 * h + 1) * WIDE : (2 * h + 2) * WIDE])
+    cw[z, c, b] = wc_in[...]
+    start = me * 24
+    low = jnp.minimum(start // LANE, WIDE // LANE - 2) * LANE
+    wide = jnp.concatenate([vec_in[...], jnp.zeros((16, LANE), F32)], axis=1)
+    vb[me] = pltpu.roll(wide, start - low, axis=1).astype(BF)
+    pl.semaphore_wait(barrier, devices - 1)
+
+    gather = Gather(place, (st, cw), gsems)
+    vsend = []
+    for d in range(1, devices):
+        other = lax.rem(me + d, devices)
+        copy = rdma(vb.at[me], vb.at[me], vsems, d, devices + d, (other // 4, other % 4))
+        copy.start()
+        vsend.append(copy)
+    gather.tick(0)
+
+    spill.wait("x")
+    for j in range(SEQS):
+        hx[j : j + 1] = u0[SPAN * j + SPAN - 16 : SPAN * j + SPAN].astype(F32)[15:16]
+    hx[SEQS:8] = jnp.zeros((8 - SEQS, WIDE), F32)
+    send_hx = line.shift(hx, hx_got, hsems.at[0], 1)
+    send_hx.start()
+    spill.wait("keep")
+    for j in range(SEQS):
+        low_keep = jnp.min(keep[SPAN * j : SPAN * (j + 1)], axis=0, keepdims=True)
+        alive[place.s, j : j + 1] = low_keep
+        alive[place.s, SEQS + j : SEQS + j + 1] = low_keep
+    send_alive = line.all(alive, asems)
+    for copy in send_alive:
+        copy.start()
+    permute_in(u0, xp, tmp)
+    spill.start("xp", xp, o_xp)
+    for d in range(1, devices):
+        other = lax.rem(me + devices - d, devices)
+        rdma(vb.at[other], vb.at[other], vsems, d, devices + d, (other // 4, other % 4)).wait_recv()
+    vec[...] = jnp.zeros_like(vec)
+    for i in range(devices):
+        w = window_of(i)
+        vec[:, w : w + WINDOW] += vb[i].astype(F32)
+    spill.start("vec", vec, o_vec)
+    gather.tick(1)
+
+    gain_a, bias_a = vec[0:1], vec[1:2]
+
+    def norm_rows(j, rows_of, gain, bias):
+        @pl.loop(0, SPAN // 16)
+        def _(t):
+            v = rows_of(pl.ds(pl.multiple_of(j * SPAN + t * 16, 16), 16))
+            xa[j, pl.ds(pl.multiple_of(8 + t * 16, 8), 16)] = unit_norm(v)[0] * gain + bias
+
+    @pl.loop(0, SEQS)
+    def _(j):
+        norm_rows(j, lambda r: xp[r].astype(F32), gain_a, bias_a)
+
+    not_first = jnp.where(place.s > 0, 1.0, 0.0).astype(F32)
+    line.shift(hx, hx_got, hsems.at[0], 1).wait_recv()
+    before = (unit_norm(hx_got[...])[0] * gain_a + bias_a) * not_first
+    for j in range(SEQS):
+        xa[j, 0:8] = first_rows(before[j : j + 1], xa[j, SPAN : SPAN + 8])
+
+    def blends(j, ratios, outs, spread_out):
+        @pl.loop(0, SPAN // 16)
+        def _(t):
+            r = pl.ds(pl.multiple_of(j * SPAN + t * 16, 16), 16)
+            prev = xa[j, pl.ds(pl.multiple_of(t * 16, 8), 16)] * spread_lanes(keep[r])
+            spread = xa[j, pl.ds(pl.multiple_of(8 + t * 16, 8), 16)] - prev
+            spread_out[r] = spread.astype(BF)
+            for ratio, out in zip(ratios, outs):
+                out[r] = (prev + spread * ratio).astype(BF)
+
+    gather.tick(2)
+
+    @pl.loop(0, SEQS)
+    def _(j):
+        blends(j, [vec[4:5], vec[5:6], vec[6:7]], [ki.at[0], ki.at[1], ki.at[2]], u0)
+
+    spill.start("ki", ki, o_ki)
+    spill.start("spa", u0, o_spa)
+    gather.tick(3)
+    spill.wait("up")
+    permute_in(u1, gyp, tmp)
+    spill.start("gyp", gyp, o_up)
+    gather.tick(4)
+    relayout(st, wd, depth, 0, 48, ((0, 0), (1, 24)))
+    relayout(st, wd, depth, 48, 32, ((2, 0),))
+    for m in range(3):
+        matmul(ki.at[m], wd.at[m], kvg.at[m])
+    spill.start("kvg", kvg, o_kvg)
+    gather.tick(5)
+
+    shrink = jnp.exp(-vec[9:10])
+    bonus = vec[10:11]
+    shrink8 = jnp.broadcast_to(shrink, (SEG, WIDE))
+    row = lax.broadcasted_iota(jnp.int32, (SEG, WIDE), 0)
+
+    @pl.loop(0, SEQS)
+    def _(j):
+        def step(s, state):
+            decay, numer, denom = state
+            r = pl.ds(pl.multiple_of(j * SPAN + s * SEG, SEG), SEG)
+            m = spread_lanes(keep[r]) * shrink8
+            ek = jnp.exp(kvg[0, r])
+            return decay * m, numer * m + ek * kvg[1, r], denom * m + ek
+
+        zero = jnp.zeros((SEG, WIDE), F32)
+        decay, numer, denom = lax.fori_loop(0, STEPS, step, (zero + 1.0, zero, zero), unroll=4)
+        for d in (1, 2, 4):
+            top = row < d
+            numer, denom, decay = (
+                numer + decay * jnp.where(top, 0.0, pltpu.roll(numer, d, axis=0)),
+                denom + decay * jnp.where(top, 0.0, pltpu.roll(denom, d, axis=0)),
+                decay * jnp.where(top, 1.0, pltpu.roll(decay, d, axis=0)),
+            )
+        states[place.s, pl.ds(j, 1)] = numer[SEG - 1 : SEG]
+        states[place.s, pl.ds(SEQS + j, 1)] = denom[SEG - 1 : SEG]
+        seg[j, 0] = jnp.where(row < 1, 1.0, pltpu.roll(decay, 1, axis=0))
+        seg[j, 1] = jnp.where(row < 1, 0.0, pltpu.roll(numer, 1, axis=0))
+        seg[j, 2] = jnp.where(row < 1, 0.0, pltpu.roll(denom, 1, axis=0))
+
+    send_states = line.all(states, ssems)
+    for copy in send_states:
+        copy.start()
+    relayout(st, wd, depth, 80, 48, ((3, 0), (4, 24)))
+    spill.start("w", wd, o_w)
+    for d in range(1, line.n):
+        src = lax.rem(place.s + line.n - d, line.n)
+        rdma(alive.at[src], alive.at[src], asems, d, line.n + d, (src, b)).wait_recv()
+        rdma(states.at[src], states.at[src], ssems, d, line.n + d, (src, b)).wait_recv()
+    spill.start("alive", alive, o_alive)
+    whole = jnp.exp(-float(SPAN) * vec[9:10])
+    arrived = jnp.zeros((SEG, WIDE), F32)
+    for src in range(7):
+        after = spread_lanes(alive[src]) * whole * arrived + states[src]
+        arrived = jnp.where(src < place.s, after, arrived)
+    carry[...] = arrived
+
+    for j in range(SEQS):
+        slot = j % 2
+        if j >= 2:
+            spill.wait(("nd", j - 2))
+        into = nd.at[slot]
+        base = j * SPAN
+        numer0 = seg[j, 0] * carry[j : j + 1] + seg[j, 1]
+        denom0 = seg[j, 0] * carry[SEQS + j : SEQS + j + 1] + seg[j, 2]
+
+        def steps(i, state):
+            numer, denom = state
+            mixes = []
+            for q in range(2):
+                lo = pl.multiple_of(i * 16 + q * 8, 8)
+                r = pl.ds(pl.multiple_of(base + lo, 8), SEG)
+                kept = spread_lanes(keep[r])
+                numer, denom = numer * kept, denom * kept
+                into[0, pl.ds(lo, SEG)] = numer
+                into[1, pl.ds(lo, SEG)] = denom
+                k, v = kvg[0, r], kvg[1, r]
+                now, ek = jnp.exp(bonus + k), jnp.exp(k)
+                wkv = (numer + now * v) / (denom + now)
+                mixes.append(sigmoid(kvg[2, r]) * wkv)
+                numer, denom = shrink8 * numer + ek * v, shrink8 * denom + ek
+            u1[pl.ds(pl.multiple_of(base + i * 16, 16), 16)] = jnp.concatenate(mixes, axis=0).astype(BF)
+            return numer, denom
+
+        lax.fori_loop(0, STEPS // 2, steps, (numer0, denom0))
+        spill.start(("nd", j), into, o_nd.at[:, pl.ds(base, SPAN)])
+        if j == 1:
+            gather.tick(6)
+    spill.start("mixed", u1, o_mixed)
+    spill.wait("kvg")
+    first = kvg.at[0]
+
+    @pl.loop(0, TOK // 256)
+    def _(i):
+        r = pl.ds(pl.multiple_of(i * 256, 256), 256)
+        first[r] = xp[r].astype(F32) + jnp.dot(u1[r], wd[3], preferred_element_type=F32)
+
+    spill.start("first", first, o_first)
+
+    @pl.loop(0, SEQS)
+    def _(j):
+        norm_rows(j, lambda r: first[r], vec[2:3], vec[3:4])
+
+    for j in range(SEQS):
+        hb[j : j + 1] = xa[j, SPAN : SPAN + 8][7:8]
+    hb[SEQS:8] = jnp.zeros((8 - SEQS, WIDE), F32)
+    send_hb = line.shift(hb, hb_got, hsems.at[1], 1)
+    send_hb.start()
+    gather.stage(0, COUNT)
+    spill.wait("ki")
+    send_hb.wait_recv()
+    before_b = hb_got[...] * not_first
+    for j in range(SEQS):
+        xa[j, 0:8] = first_rows(before_b[j : j + 1], xa[j, SPAN : SPAN + 8])
+
+    @pl.loop(0, SEQS)
+    def _(j):
+        blends(j, [vec[7:8], vec[8:9]], [ki.at[0], ki.at[1]], spb)
+
+    spill.start("spb", spb, o_spb)
+    spill.start("ei", ki.at[0], o_ei)
+    spill.start("si", ki.at[1], o_si)
+    sig = kvg.at[1]
+
+    @pl.loop(0, TOK // 256)
+    def _(i):
+        r = pl.ds(pl.multiple_of(i * 256, 256), 256)
+        chosen = sigmoid(jnp.dot(ki[1, r], wd[4], preferred_element_type=F32))
+        sig[r] = chosen
+        ki[2, r] = (gyp[r].astype(F32) * chosen).astype(BF)
+
+    spill.start("gc", ki.at[2], o_gc)
+    relayout(st, we, depth, 128, 48, ((0, 0), (1, 24)))
+    gather.tick(7)
+    relayout(st, we, depth, 176, 48, ((2, 0), (3, 24)))
+    spill.start("e", we, o_e)
+    for k in range(4):
+        gather.stage(5, k)
+
+    def square(f):
+        @pl.loop(0, depth)
+        def _(i):
+            r = pl.ds(pl.multiple_of(i * 256, 256), 256)
+            positive = jnp.maximum(jnp.dot(ki[0, r], we[f], preferred_element_type=F32), 0.0)
+            st[i, :, :, 96 + 32 * f : 128 + 32 * f] = (positive * positive).astype(BF).reshape(2, 4, 32, WIDE)
+
+    def contract_grad(f):
+        left = st[:, :, :, 96 + 32 * f : 128 + 32 * f].reshape(TOK, WIDE)
+        for h in range(2):
+            got = lax.dot_general(left[:, 384 * h : 384 * (h + 1)], ki[2], (((0,), (0,)), ((), ())), preferred_element_type=F32)
+            st[f, h, :, 0:96] = got.astype(BF).reshape(4, 96, WIDE)
+
+    square(0)
+    square(1)
+    gather.tick(8)
+    square(2)
+    square(3)
+    contract_grad(0)
+    contract_grad(1)
+    gather.tick(9)
+    spill.start("c", cw, o_c)
+    contract_grad(2)
+    contract_grad(3)
+    spill.start("pkc", st.at[:, :, :, pl.ds(0, 96)], o_pkc)
+    spill.start("sq", st.at[:, :, :, pl.ds(96, 128)], o_sq)
+    spill.wait("mixed", "spa")
+
+    @pl.loop(0, depth)
+    def _(i):
+        r = pl.ds(pl.multiple_of(i * 256, 256), 256)
+        total = jnp.zeros((256, WIDE), F32)
+        for f in range(4):
+            part = st[i, :, :, 96 + 32 * f : 128 + 32 * f].reshape(256, WIDE)
+            total = total + jnp.dot(part, cw[f].reshape(WIDE, WIDE), preferred_element_type=F32)
+        chosen = sig[r]
+        u1[r] = (first[r] + chosen * total).astype(BF)
+        u0[r] = (gyp[r].astype(F32) * total * chosen * (1.0 - chosen)).astype(BF)
+
+    spill.start("gs", u0, o_gs)
+    spill.start("bo", u1, o_bo)
+    for copy in vsend + send_alive + send_states + [send_hx, send_hb]:
+        copy.wait_send()
+    for k in range(4, COUNT):
+        gather.stage(5, k)
+    spill.wait()
+
+
+def forward_call(x, keep, up, vec, shards, depth):
+    hbm, vmem = pl.BlockSpec(memory_space=pl.ANY), pl.BlockSpec(memory_space=pltpu.VMEM)
+    s = jax.ShapeDtypeStruct
+    seq = depth * 2
+    devices = depth * 8
+    rows = (TOK, WIDE)
+    outs = dict(
+        w=s((5, WIDE, WIDE), BF), e=s((4, WIDE, WIDE), BF), c=s((depth, 2, 4, 96, WIDE), BF), ki=s((3,) + rows, BF),
+        spa=s(rows, BF), spb=s(rows, BF), mixed=s(rows, BF), ei=s(rows, BF), si=s(rows, BF), gc=s(rows, BF), gs=s(rows, BF),
+        xp=s(rows, BF), up=s(rows, BF), sq=s((depth, 2, 4, 128, WIDE), BF), pkc=s((depth, 2, 4, 96, WIDE), BF),
+        kvg=s((3,) + rows, F32), nd=s((2,) + rows, F32), first=s(rows, F32), vec=s((16, WIDE), F32), alive=s((seq, 8, LANE), F32),
+        bo=s(rows, BF))
+    scratch = [
+        pltpu.VMEM((depth, 2, 4, ROWS_MAIN, WIDE), BF), pltpu.VMEM((depth, 2, 4, ROWS_LAST, WIDE), BF),
+        pltpu.VMEM((5, WIDE, WIDE), BF), pltpu.VMEM((4, WIDE, WIDE), BF),
+        pltpu.VMEM(rows, BF), pltpu.VMEM(rows, BF), pltpu.VMEM(rows, BF), pltpu.VMEM(rows, BF),
+        pltpu.VMEM((6, SPAN, LANE), F32), pltpu.VMEM((TOK, LANE), F32), pltpu.VMEM((SEQS, SPAN + 8, WIDE), F32),
+        pltpu.VMEM((3,) + rows, BF), pltpu.VMEM((3,) + rows, F32), pltpu.VMEM((2, 2, SPAN, WIDE), F32), pltpu.VMEM(rows, BF),
+        pltpu.VMEM((devices, 16, WINDOW), BF), pltpu.VMEM((16, WIDE), F32), pltpu.VMEM((seq, 8, WIDE), F32), pltpu.VMEM((seq, 8, LANE), F32),
+        pltpu.VMEM((SEQS, 3, SEG, WIDE), F32), pltpu.VMEM((8, WIDE), F32),
+        pltpu.VMEM((8, WIDE), F32), pltpu.VMEM((8, WIDE), F32), pltpu.VMEM((8, WIDE), F32), pltpu.VMEM((8, WIDE), F32),
+        pltpu.SemaphoreType.DMA((COUNT, 22)), pltpu.SemaphoreType.DMA((2 * devices,)), pltpu.SemaphoreType.DMA((2 * seq,)),
+        pltpu.SemaphoreType.DMA((2 * seq,)), pltpu.SemaphoreType.DMA((2, 2)), pltpu.SemaphoreType.DMA((32,)),
+    ]
+    got = pl.pallas_call(
+        forward_kernel,
+        out_shape=tuple(outs.values()),
+        in_specs=[hbm, hbm, hbm] + [vmem] * 8,
+        out_specs=tuple(hbm for _ in outs),
+        scratch_shapes=scratch,
+        compiler_params=pltpu.CompilerParams(collective_id=0, has_side_effects=True, vmem_limit_bytes=62 << 20),
+        cost_estimate=pl.CostEstimate(flops=2 * 1024 * 12 * 768 * 768, bytes_accessed=60 << 20, transcendentals=0),
+    )(x, keep, up, vec, *shards)
+    return dict(zip(outs, got))
+
+
+NT = (((1,), (1,)), ((), ()))
+TN = (((0,), (0,)), ((), ()))
+
+
+def backward_kernel(i_w, i_e, i_c, i_ki, i_spa, i_spb, i_mixed, i_ei, i_si, i_gc, i_gs, i_xp, i_up, i_sq, i_pkc, i_kvg, i_nd, i_first, i_vec,
+                    i_alive, i_keep,
+                    o_out, o_tokens, o_vec,
+                    main, last, from_core, near, diag, lines, out, we, cw, p, q, xg, keep, vec, alive, states, seg, vg, vr, hx, hx_got, hb, hb_got,
+                    rsems, credits, ssems, hsems, zsems, lsems):
+    place = Place()
+    line = Line(place)
+    depth = place.depth
+    z, c, b = place.z, place.c, place.b
+    spill = Spill(lsems)
+    spill.start("pkc", i_pkc, last)
+    spill.start("cw", i_c, cw)
+    spill.start("keep", i_keep, keep)
+    spill.start("vec", i_vec, vec)
+    spill.start("alive", i_alive, alive)
+    spill.start("we", i_e, we)
+    barrier = pltpu.get_barrier_semaphore()
+    peers = [place.x, place.y] + [(lax.rem(place.s + d, line.n), b) for d in range(1, line.n)]
+    for peer in peers:
+        pl.semaphore_signal(barrier, inc=1, device_id=peer, device_id_type=MESH)
+    pl.semaphore_wait(barrier, len(peers))
+    scatter = Scatter(place, (main, last), from_core, near, diag, lines, out, rsems, credits)
+    run = scatter.stage
+    vg[...] = jnp.zeros_like(vg)
+    not_last = jnp.where(place.s < line.n - 1, 1.0, 0.0).astype(F32)
+
+    def pack(first, second, r0):
+        @pl.loop(0, depth * 2)
+        def _(i):
+            rows = pl.ds(pl.multiple_of(i * 96, 96), 96)
+            u = first[rows].astype(F32)
+            v = None if second is None else second[rows].astype(F32)
+            for k in range(4):
+                mine = u[24 * k : 24 * k + 24]
+                other = jnp.zeros((8, WIDE), F32) if v is None else v[24 * k : 24 * k + 24]
+                joined = jnp.concatenate([mine, other], axis=0)
+                main[i // 2, i % 2, k, r0 : r0 + joined.shape[0]] = joined.astype(BF)
+
+    def outer(left, right, into):
+        for h in range(2):
+            cols = slice(384 * h, 384 * h + 384)
+            into[cols] = lax.dot_general(left[:, cols], right[...], TN, preferred_element_type=F32).astype(BF)
+
+    def fold(v):
+        return v[0:8] + v[8:16]
+
+    def following_rows(halo):
+        for j in range(SEQS):
+            moved = pltpu.roll(xg[j, 0:8], SEG - 1, axis=0)
+            at_end = lax.broadcasted_iota(jnp.int32, moved.shape, 0) == SEG - 1
+            xg[j, SPAN : SPAN + 8] = jnp.where(at_end, halo[j : j + 1], moved)
+
+    def send_first(src, dst, sems):
+        for j in range(SEQS):
+            src[j : j + 1] = xg[j, 0:8][0:1]
+        src[SEQS:8] = jnp.zeros((8 - SEQS, WIDE), F32)
+        copy = line.shift(src, dst, sems, -1)
+        copy.start()
+        return copy
+
+    def norm_back(rows, gain, source, gain_at, bias_at, finish):
+        @pl.loop(0, SEQS)
+        def _(j):
+            def tile(t, sums):
+                r = pl.ds(pl.multiple_of(j * SPAN + t * 16, 16), 16)
+                grad = rows[r] + xg[j, pl.ds(pl.multiple_of(t * 16 + 8, 8), 16)]
+                unit, factor = unit_norm(source(r))
+                h = grad * gain
+                back = factor * (h - jnp.mean(h, axis=-1, keepdims=True) - unit * jnp.mean(h * unit, axis=-1, keepdims=True))
+                finish(r, back)
+                return sums[0] + fold(grad * unit), sums[1] + fold(grad)
+
+            zero = jnp.zeros((8, WIDE), F32)
+            sums = lax.fori_loop(0, SPAN // 16, tile, (zero, zero))
+            vg[gain_at] += sums[0]
+            vg[bias_at] += sums[1]
+
+    def channel_mix(gc, ei, si, gs, sqb, ge, gt):
+        load = lambda f: spill.start(("sq", f), i_sq.at[:, :, :, pl.ds(32 * f, 32)], sqb.at[f % 2])
+        spill.start("gc", i_gc, gc)
+        load(0)
+        load(1)
+        spill.start("ei", i_ei, ei)
+        spill.start("si", i_si, si)
+        spill.start("gs", i_gs, gs)
+        spill.wait("pkc")
+        run(0, 0)
+        run(0, 1)
+        spill.wait("cw", "gc")
+
+        def expand_back(f):
+            spill.wait(("sq", f))
+
+            @pl.loop(0, TOK // 256)
+            def _(i):
+                r = pl.ds(pl.multiple_of(i * 256, 256), 256)
+                grad = lax.dot_general(gc[r], cw[f].reshape(WIDE, WIDE), NT, preferred_element_type=F32)
+                positive = jnp.sqrt(sqb[f % 2, i].reshape(256, WIDE).astype(F32))
+                ge[r] = (2.0 * positive * grad).astype(BF)
+
+            if f + 2 < 4:
+                load(f + 2)
+
+        def expand_in_back(f):
+            @pl.loop(0, TOK // 512)
+            def _(i):
+                r = pl.ds(pl.multiple_of(i * 512, 512), 512)
+                got = lax.dot_general(ge[r], we[f], NT, preferred_element_type=F32)
+                p[r] = got if f == 0 else p[r] + got
+
+        expand_back(0)
+        run(1, 0)
+        spill.wait("ei", "we")
+        outer(ei, ge, gt.at[0])
+        run(1, 1)
+        run(2, 0)
+        expand_in_back(0)
+        spill.start("ws", i_w.at[4], we.at[0])
+        expand_back(1)
+        run(2, 1)
+        run(3, 0)
+        outer(ei, ge, gt.at[1])
+        pack(gt.at[0], gt.at[1], 128)
+        run(0, 2)
+        expand_in_back(1)
+        spill.start("wo", i_w.at[3], we.at[1])
+        run(3, 1)
+        run(4, 0)
+        run(1, 2)
+        expand_back(2)
+        run(2, 2)
+        outer(ei, ge, gt.at[0])
+        run(4, 1)
+        expand_in_back(2)
+        expand_back(3)
+        outer(ei, ge, gt.at[1])
+        pack(gt.at[0], gt.at[1], 176)
+        run(0, 3)
+        run(3, 2)
+        expand_in_back(3)
+        run(1, 3)
+        spill.wait("si", "gs", "ws", "wo")
+        spill.start("wk", i_w.at[0], we.at[2])
+        spill.start("wv", i_w.at[1], we.at[3])
+        spill.start("spb", i_spb, gc)
+        outer(si, gs, gt.at[1])
+        run(2, 3)
+        run(4, 2)
+
+        @pl.loop(0, TOK // 512)
+        def _(i):
+            r = pl.ds(pl.multiple_of(i * 512, 512), 512)
+            q[r] = lax.dot_general(gs[r], we[0], NT, preferred_element_type=F32)
+
+        spill.start("wr", i_w.at[2], we.at[0])
+        spill.start("gyp", i_up, ge)
+        spill.start("mixed", i_mixed, ei)
+        spill.wait("keep", "vec", "spb")
+        run(3, 3)
+        re, rs = vec[7:8], vec[8:9]
+
+        @pl.loop(0, SEQS)
+        def _(j):
+            def tile(t, sums):
+                r = pl.ds(pl.multiple_of(j * SPAN + t * 16, 16), 16)
+                ge_in, gs_in, spread = p[r], q[r], gc[r].astype(F32)
+                xg[j, pl.ds(pl.multiple_of(t * 16, 16), 16)] = (ge_in * (1.0 - re) + gs_in * (1.0 - rs)) * spread_lanes(keep[r])
+                p[r] = ge_in * re + gs_in * rs
+                return sums[0] + fold(ge_in * spread), sums[1] + fold(gs_in * spread)
+
+            zero = jnp.zeros((8, WIDE), F32)
+            sums = lax.fori_loop(0, SPAN // 16, tile, (zero, zero))
+            vg[7] += sums[0]
+            vg[8] += sums[1]
+
+        send = send_first(hb, hb_got, hsems.at[0])
+        spill.start("first", i_first, q)
+        run(4, 3)
+        spill.wait("gyp", "mixed", "first")
+        send.wait_recv()
+        following_rows(hb_got[...] * not_last)
+
+        def finish(r, back):
+            grad = ge[r].astype(F32) + back
+            p[r] = grad
+            si[r] = grad.astype(BF)
+
+        norm_back(p, vec[2:3], lambda r: q[r], 2, 3, finish)
+        send.wait_send()
+        outer(ei, si, gt.at[0])
+        pack(gt.at[0], gt.at[1], 80)
+        run(0, 4)
+
+        @pl.loop(0, TOK // 512)
+        def _(i):
+            r = pl.ds(pl.multiple_of(i * 512, 512), 512)
+            q[r] = lax.dot_general(si[r], we[1], NT, preferred_element_type=F32)
+
+        spill.wait("wk", "wv", "wr")
+
+    unit = pltpu.VMEM((TOK, WIDE), BF)
+    pl.run_scoped(channel_mix, unit, unit, unit, unit, pltpu.VMEM((2, depth, 2, 4, 32, WIDE), BF), unit,
+                  pltpu.VMEM((2, WIDE, WIDE), BF))
+    run(1, 4)
+    spill.wait("alive")
+    shrink = jnp.exp(-vec[9:10])
+    shrink8 = jnp.broadcast_to(shrink, (SEG, WIDE))
+    bonus = vec[10:11]
+    row = lax.broadcasted_iota(jnp.int32, (SEG, WIDE), 0)
+    zero = jnp.zeros((SEG, WIDE), F32)
+
+    def time_mix(gkvg):
+        def sweeps(buf):
+            def load(j, name):
+                spill.start((name, "kvg", j), i_kvg.at[:, pl.ds(j * SPAN, SPAN)], buf.at[j % 2, pl.ds(0, 3)])
+                spill.start((name, "nd", j), i_nd.at[:, pl.ds(j * SPAN, SPAN)], buf.at[j % 2, pl.ds(3, 2)])
+
+            def arrive(j, name):
+                spill.wait((name, "kvg", j), (name, "nd", j))
+
+            load(0, 1)
+            load(1, 1)
+            for j in range(SEQS):
+                arrive(j, 1)
+                at = buf.at[j % 2]
+
+                def back(i, state):
+                    decay, numer, denom, bonus_sum = state
+                    gates = [None, None]
+                    for h in (1, 0):
+                        lo = pl.multiple_of((STEPS // 2 - 1 - i) * 16 + 8 * h, 8)
+                        r = pl.ds(pl.multiple_of(j * SPAN + lo, 8), SEG)
+                        here = pl.ds(lo, SEG)
+                        kept = spread_lanes(keep[r])
+                        k, v = at[0, here], at[1, here]
+                        now = jnp.exp(bonus + k)
+                        inverse = 1.0 / (at[4, here] + now)
+                        wkv = (at[3, here] + now * v) * inverse
+                        s = sigmoid(at[2, here])
+                        gm = q[r]
+                        gw = gm * s
+                        gates[h] = gw * wkv * (1.0 - s)
+                        dn = gw * inverse
+                        dd = -dn * wkv
+                        q[r] = dn
+                        bonus_sum = bonus_sum + now * (dn * v + dd)
+                        m = kept * shrink8
+                        decay, numer, denom = decay * m, numer * m + kept * dn, denom * m + kept * dd
+                    rows = pl.ds(pl.multiple_of(j * SPAN + (STEPS // 2 - 1 - i) * 16, 16), 16)
+                    gkvg[2, rows] = jnp.concatenate(gates, axis=0).astype(BF)
+                    return decay, numer, denom, bonus_sum
+
+                decay, numer, denom, bonus_sum = lax.fori_loop(0, STEPS // 2, back, (zero + 1.0, zero, zero, zero))
+                load(j + 2, 1) if j + 2 < SEQS else load(j - 2, 2)
+                vg[10] += bonus_sum
+                for d in (1, 2, 4):
+                    end = row >= SEG - d
+                    numer, denom, decay = (
+                        numer + decay * jnp.where(end, 0.0, pltpu.roll(numer, SEG - d, axis=0)),
+                        denom + decay * jnp.where(end, 0.0, pltpu.roll(denom, SEG - d, axis=0)),
+                        decay * jnp.where(end, 1.0, pltpu.roll(decay, SEG - d, axis=0)),
+                    )
+                states[place.s, j : j + 1] = numer[0:1]
+                states[place.s, SEQS + j : SEQS + j + 1] = denom[0:1]
+                end = row >= SEG - 1
+                seg[j, 0] = jnp.where(end, 1.0, pltpu.roll(decay, SEG - 1, axis=0))
+                seg[j, 1] = jnp.where(end, 0.0, pltpu.roll(numer, SEG - 1, axis=0))
+                seg[j, 2] = jnp.where(end, 0.0, pltpu.roll(denom, SEG - 1, axis=0))
+                if j == 1:
+                    run(2, 4)
+            sent = line.all(states, ssems)
+            for copy in sent:
+                copy.start()
+            run(3, 4)
+            for d in range(1, line.n):
+                src = lax.rem(place.s + line.n - d, line.n)
+                rdma(states.at[src], states.at[src], ssems, d, line.n + d, (src, b)).wait_recv()
+            whole = jnp.exp(-float(SPAN) * vec[9:10])
+            arrived = zero
+            for src in range(7, 0, -1):
+                after = spread_lanes(alive[src]) * whole * arrived + states[src]
+                arrived = jnp.where(src > place.s, after, arrived)
+            for j in range(SEQS):
+                arrive(j, 2)
+                at = buf.at[j % 2]
+                numer0 = seg[j, 0] * arrived[j : j + 1] + seg[j, 1]
+                denom0 = seg[j, 0] * arrived[SEQS + j : SEQS + j + 1] + seg[j, 2]
+
+                def back(i, state):
+                    an, ad, decay_sum = state
+                    keys, values = [None, None], [None, None]
+                    for h in (1, 0):
+                        lo = pl.multiple_of((STEPS // 2 - 1 - i) * 16 + 8 * h, 8)
+                        r = pl.ds(pl.multiple_of(j * SPAN + lo, 8), SEG)
+                        here = pl.ds(lo, SEG)
+                        kept = spread_lanes(keep[r])
+                        k, v, numer, denom = at[0, here], at[1, here], at[3, here], at[4, here]
+                        now, ek = jnp.exp(bonus + k), jnp.exp(k)
+                        wkv = (numer + now * v) / (denom + now)
+                        dn = q[r]
+                        dd = -dn * wkv
+                        keys[h] = ek * (an * v + ad) + now * (dn * v + dd)
+                        values[h] = ek * an + now * dn
+                        decay_sum = decay_sum + an * numer + ad * denom
+                        an, ad = kept * (dn + shrink8 * an), kept * (dd + shrink8 * ad)
+                    rows = pl.ds(pl.multiple_of(j * SPAN + (STEPS // 2 - 1 - i) * 16, 16), 16)
+                    gkvg[0, rows] = jnp.concatenate(keys, axis=0).astype(BF)
+                    gkvg[1, rows] = jnp.concatenate(values, axis=0).astype(BF)
+                    return an, ad, decay_sum
+
+                _, _, decay_sum = lax.fori_loop(0, STEPS // 2, back, (numer0, denom0, zero))
+                if j + 2 < SEQS:
+                    load(j + 2, 2)
+                vg[9] += -shrink * decay_sum
+            for copy in sent:
+                copy.wait_send()
+            run(4, 4)
+
+        pl.run_scoped(sweeps, pltpu.VMEM((2, 5, SPAN, WIDE), F32))
+
+        def mixes(ki, spa, gt, parts):
+            spill.start("ki0", i_ki.at[0], ki.at[0])
+            spill.start("ki1", i_ki.at[1], ki.at[1])
+            spill.start("spa", i_spa, spa)
+            spill.wait("ki0")
+            outer(ki.at[0], gkvg.at[0], gt.at[0])
+            spill.start("ki2", i_ki.at[2], ki.at[0])
+            spill.wait("ki1")
+            outer(ki.at[1], gkvg.at[1], gt.at[1])
+            spill.start("xp", i_xp, ki.at[1])
+            pack(gt.at[0], gt.at[1], 0)
+            spill.wait("ki2")
+            outer(ki.at[0], gkvg.at[2], gt.at[0])
+            pack(gt.at[0], None, 48)
+            run(0, 5)
+            spill.wait("spa")
+            ratios = [vec[4 + m : 5 + m] for m in range(3)]
+            for j in range(SEQS):
+                rows = pl.ds(j * SPAN, SPAN)
+                for m, w in enumerate((we.at[2], we.at[3], we.at[0])):
+                    parts[m] = lax.dot_general(gkvg[m, rows], w[...], NT, preferred_element_type=F32)
+
+                def tile(t, sums):
+                    r = pl.ds(pl.multiple_of(j * SPAN + t * 16, 16), 16)
+                    here = pl.ds(pl.multiple_of(t * 16, 16), 16)
+                    spread = spa[r].astype(F32)
+                    g = [parts[m, here] for m in range(3)]
+                    shifted = g[0] * (1.0 - ratios[0]) + g[1] * (1.0 - ratios[1]) + g[2] * (1.0 - ratios[2])
+                    xg[j, here] = shifted * spread_lanes(keep[r])
+                    q[r] = g[0] * ratios[0] + g[1] * ratios[1] + g[2] * ratios[2]
+                    return tuple(s + fold(v * spread) for s, v in zip(sums, g))
+
+                sums = lax.fori_loop(0, SPAN // 16, tile, (zero, zero, zero))
+                for m in range(3):
+                    vg[4 + m] += sums[m]
+                if j == 0:
+                    run(1, 5)
+                if j == 2:
+                    run(2, 5)
+            send = send_first(hx, hx_got, hsems.at[1])
+            spill.wait("xp")
+            send.wait_recv()
+            following_rows(hx_got[...] * not_last)
+
+            def finish(r, back):
+                p[r] = p[r] + back
+
+            norm_back(q, vec[0:1], lambda r: ki[1, r].astype(F32), 0, 1, finish)
+            send.wait_send()
+
+        unit2 = pltpu.VMEM((2, TOK, WIDE), BF)
+        pl.run_scoped(mixes, unit2, unit, pltpu.VMEM((2, WIDE, WIDE), BF), pltpu.VMEM((3, SPAN, WIDE), F32))
+
+    pl.run_scoped(time_mix, pltpu.VMEM((3, TOK, WIDE), BF))
+    spill.start("tokens", p, o_tokens)
+    vr[0, VECTORS:16] = jnp.zeros((16 - VECTORS, WIDE), F32)
+    for i in range(VECTORS):
+        vr[0, i : i + 1] = jnp.sum(vg[i], axis=0, keepdims=True)
+
+    def exchange(src, slot, to):
+        copy = rdma(vr.at[src], vr.at[slot], zsems.at[slot], 0, 1, to)
+        copy.start()
+        return copy
+
+    one = exchange(0, 1, place.core)
+    one.wait_recv()
+    vr[2] = vr[0] + vr[1]
+    two = exchange(2, 3, place.x)
+    run(3, 5)
+    two.wait_recv()
+    vr[4] = vr[2] + vr[3]
+    three = exchange(4, 5, place.y)
+    three.wait_recv()
+    vr[6] = vr[4] + vr[5]
+    four = [exchange(6, 6 + d, place.along(d)[1]) for d in range(1, depth)]
+    run(4, 5)
+    total = vr[6]
+    for d in range(1, depth):
+        four[d - 1].wait_recv()
+        total = total + vr[6 + d]
+    vr[6 + depth] = total
+    me = place.s * 4 + place.b
+    start = me * 24
+    low = pl.multiple_of(jnp.minimum(start // LANE, WIDE // LANE - 2) * LANE, LANE)
+    mine = vr[6 + depth, :, pl.ds(low, WINDOW)]
+    o_vec[...] = pltpu.roll(mine, WINDOW - (start - low), axis=1)[:, 0:LANE]
+    spill.start("out", out, o_out)
+    for copy in [one, two, three] + four:
+        copy.wait_send()
+    for k in range(COUNT):
+        run(5, k)
+    spill.wait()
+
+
+BACK_INPUTS = ("w", "e", "c", "ki", "spa", "spb", "mixed", "ei", "si", "gc", "gs", "xp", "up", "sq", "pkc", "kvg", "nd", "first", "vec", "alive")
+
+
+def backward_call(f, keep, depth):
+    hbm, vmem = pl.BlockSpec(memory_space=pl.ANY), pl.BlockSpec(memory_space=pltpu.VMEM)
+    s = jax.ShapeDtypeStruct
+    seq, rows = depth * 2, ROWS_MAIN + ROWS_LAST
+    top = max(n for _, _, n, _ in SCATTER_CHUNKS)
+    row8 = pltpu.VMEM((8, WIDE), F32)
+    return pl.pallas_call(
+        backward_kernel,
+        out_shape=(s((rows, WIDE), F32), s((TOK, WIDE), F32), s((16, LANE), F32)),
+        in_specs=[hbm] * (len(BACK_INPUTS) + 1),
+        out_specs=(hbm, hbm, vmem),
+        scratch_shapes=[
+            pltpu.VMEM((depth, 2, 4, ROWS_MAIN, WIDE), BF), pltpu.VMEM((depth, 2, 4, ROWS_LAST, WIDE), BF),
+            pltpu.VMEM((2, depth, 4, top, WIDE), BF), pltpu.VMEM((2, 2, depth, top, WIDE), BF), pltpu.VMEM((2, depth, top, WIDE), BF),
+            pltpu.VMEM((depth - 1, rows, WIDE), BF), pltpu.VMEM((rows, WIDE), F32),
+            pltpu.VMEM((4, WIDE, WIDE), BF), pltpu.VMEM((depth, 2, 4, 96, WIDE), BF),
+            pltpu.VMEM((TOK, WIDE), F32), pltpu.VMEM((TOK, WIDE), F32), pltpu.VMEM((SEQS, SPAN + 8, WIDE), F32),
+            pltpu.VMEM((TOK, LANE), F32), pltpu.VMEM((16, WIDE), F32), pltpu.VMEM((seq, 8, LANE), F32), pltpu.VMEM((seq, 8, WIDE), F32),
+            pltpu.VMEM((SEQS, 3, SEG, WIDE), F32), pltpu.VMEM((VECTORS, 8, WIDE), F32), pltpu.VMEM((7 + depth, 16, WIDE), F32),
+            row8, row8, row8, row8,
+            pltpu.SemaphoreType.DMA((COUNT, 16)), pltpu.SemaphoreType.REGULAR((5,)), pltpu.SemaphoreType.DMA((2 * seq,)),
+            pltpu.SemaphoreType.DMA((2, 2)), pltpu.SemaphoreType.DMA((7 + depth, 2)), pltpu.SemaphoreType.DMA((56,)),
+        ],
+        compiler_params=pltpu.CompilerParams(collective_id=1, has_side_effects=True, vmem_limit_bytes=62 << 20),
+        cost_estimate=pl.CostEstimate(flops=2 * 1024 * 26 * 768 * 768, bytes_accessed=60 << 20, transcendentals=0),
+    )(*[f[n] for n in BACK_INPUTS], keep)
+
+
+def fast_body(layer_inputs, document_openings, wk, wv, wr, wo, we, ws, wc, *rest):
+    vectors, upstream = rest[:VECTORS], rest[VECTORS]
+    depth = lax.axis_size("seq") // 2
+    keep = 1.0 - document_openings.astype(F32)
+    keep = keep.reshape(SEQS, SEG, STEPS).transpose(0, 2, 1).reshape(TOK, 1)
+    keep = jnp.broadcast_to(keep, (TOK, LANE))
+    vec = jnp.pad(jnp.stack(vectors).astype(F32), ((0, 16 - VECTORS), (0, LANE - 24)))
+    got = forward_call(layer_inputs.reshape(TOK, WIDE), keep, upstream.reshape(TOK, WIDE), vec, (wk, wv, wr, wo, ws, we, wc), depth)
+    out, tokens, small = backward_call(got, keep, depth)
+
+    def natural(v):
+        return v.reshape(SEQS, STEPS, SEG, WIDE).transpose(0, 2, 1, 3).reshape(SEQS, SPAN, WIDE)
+
+    expand = jnp.concatenate([out[128 + 24 * i : 152 + 24 * i] for i in range(4)], axis=1)
+    return (natural(got["bo"]), natural(tokens), out[0:24], out[24:48], out[48:72], out[80:104], expand, out[104:128], out[224:320]) + tuple(
+        small[i, 0:24] for i in range(VECTORS))
 
 
 def from_behind(block, axis, distance):
@@ -143,24 +1253,24 @@
     upstream_adjoint,
 ):
     gathered = (
-        lax.all_gather(mixing_lookup_projection, ("seq", "batch"), axis=0, tiled=True),
-        lax.all_gather(mixing_payload_projection, ("seq", "batch"), axis=0, tiled=True),
-        lax.all_gather(mixing_acceptor_projection, ("seq", "batch"), axis=0, tiled=True),
-        lax.all_gather(mixing_result_projection, ("seq", "batch"), axis=0, tiled=True),
-        lax.all_gather(feedforward_lookup_projection, ("seq", "batch"), axis=0, tiled=True),
-        lax.all_gather(feedforward_acceptor_projection, ("seq", "batch"), axis=0, tiled=True),
-        lax.all_gather(feedforward_payload_projection, ("seq", "batch"), axis=0, tiled=True),
-        lax.all_gather(premix_layer_scaling, ("seq", "batch"), axis=0, tiled=True),
-        lax.all_gather(premix_layer_offset, ("seq", "batch"), axis=0, tiled=True),
-        lax.all_gather(postmix_layer_scaling, ("seq", "batch"), axis=0, tiled=True),
-        lax.all_gather(postmix_layer_offset, ("seq", "batch"), axis=0, tiled=True),
-        lax.all_gather(mixing_lookup_blend, ("seq", "batch"), axis=0, tiled=True),
-        lax.all_gather(mixing_payload_blend, ("seq", "batch"), axis=0, tiled=True),
-        lax.all_gather(mixing_acceptor_blend, ("seq", "batch"), axis=0, tiled=True),
-        lax.all_gather(feedforward_lookup_blend, ("seq", "batch"), axis=0, tiled=True),
-        lax.all_gather(feedforward_acceptor_blend, ("seq", "batch"), axis=0, tiled=True),
-        lax.all_gather(feature_fading_speed, ("seq", "batch"), axis=0, tiled=True),
-        lax.all_gather(present_token_reward, ("seq", "batch"), axis=0, tiled=True),
+        lax.all_gather(mixing_lookup_projection, BOTH, axis=0, tiled=True),
+        lax.all_gather(mixing_payload_projection, BOTH, axis=0, tiled=True),
+        lax.all_gather(mixing_acceptor_projection, BOTH, axis=0, tiled=True),
+        lax.all_gather(mixing_result_projection, BOTH, axis=0, tiled=True),
+        lax.all_gather(feedforward_lookup_projection, BOTH, axis=0, tiled=True),
+        lax.all_gather(feedforward_acceptor_projection, BOTH, axis=0, tiled=True),
+        lax.all_gather(feedforward_payload_projection, BOTH, axis=0, tiled=True),
+        lax.all_gather(premix_layer_scaling, BOTH, axis=0, tiled=True),
+        lax.all_gather(premix_layer_offset, BOTH, axis=0, tiled=True),
+        lax.all_gather(postmix_layer_scaling, BOTH, axis=0, tiled=True),
+        lax.all_gather(postmix_layer_offset, BOTH, axis=0, tiled=True),
+        lax.all_gather(mixing_lookup_blend, BOTH, axis=0, tiled=True),
+        lax.all_gather(mixing_payload_blend, BOTH, axis=0, tiled=True),
+        lax.all_gather(mixing_acceptor_blend, BOTH, axis=0, tiled=True),
+        lax.all_gather(feedforward_lookup_blend, BOTH, axis=0, tiled=True),
+        lax.all_gather(feedforward_acceptor_blend, BOTH, axis=0, tiled=True),
+        lax.all_gather(feature_fading_speed, BOTH, axis=0, tiled=True),
+        lax.all_gather(present_token_reward, BOTH, axis=0, tiled=True),
     )
     full_key, full_value, full_gate, full_output, full_expand, full_select, full_contract = (
         gathered[:7]
@@ -238,13 +1348,13 @@
     select_sig = jax.nn.sigmoid(selected)
     block_out = (first + select_sig * contracted).astype(jnp.bfloat16)
     again = (
-        lax.all_gather(mixing_lookup_projection, ("seq", "batch"), axis=0, tiled=True),
-        lax.all_gather(mixing_payload_projection, ("seq", "batch"), axis=0, tiled=True),
-        lax.all_gather(mixing_acceptor_projection, ("seq", "batch"), axis=0, tiled=True),
-        lax.all_gather(mixing_result_projection, ("seq", "batch"), axis=0, tiled=True),
-        lax.all_gather(feedforward_lookup_projection, ("seq", "batch"), axis=0, tiled=True),
-        lax.all_gather(feedforward_acceptor_projection, ("seq", "batch"), axis=0, tiled=True),
-        lax.all_gather(feedforward_payload_projection, ("seq", "batch"), axis=0, tiled=True),
+        lax.all_gather(mixing_lookup_projection, BOTH, axis=0, tiled=True),
+        lax.all_gather(mixing_payload_projection, BOTH, axis=0, tiled=True),
+        lax.all_gather(mixing_acceptor_projection, BOTH, axis=0, tiled=True),
+        lax.all_gather(mixing_result_projection, BOTH, axis=0, tiled=True),
+        lax.all_gather(feedforward_lookup_projection, BOTH, axis=0, tiled=True),
+        lax.all_gather(feedforward_acceptor_projection, BOTH, axis=0, tiled=True),
+        lax.all_gather(feedforward_payload_projection, BOTH, axis=0, tiled=True),
     )
     full_key, full_value, full_gate, full_output, full_expand, full_select, full_contract = again
     upstream = upstream_adjoint.astype(jnp.float32)
@@ -330,24 +1440,24 @@
     )
     tokens_grad = grad_first + grad_from_a
     shares = (
-        lax.psum_scatter(key_grad, ("seq", "batch"), scatter_dimension=0, tiled=True),
-        lax.psum_scatter(value_grad, ("seq", "batch"), scatter_dimension=0, tiled=True),
-        lax.psum_scatter(gate_grad, ("seq", "batch"), scatter_dimension=0, tiled=True),
-        lax.psum_scatter(output_grad, ("seq", "batch"), scatter_dimension=0, tiled=True),
-        lax.psum_scatter(expand_grad, ("seq", "batch"), scatter_dimension=0, tiled=True),
-        lax.psum_scatter(select_grad, ("seq", "batch"), scatter_dimension=0, tiled=True),
-        lax.psum_scatter(contract_grad, ("seq", "batch"), scatter_dimension=0, tiled=True),
-        lax.psum_scatter(attn_gain_grad, ("seq", "batch"), scatter_dimension=0, tiled=True),
-        lax.psum_scatter(attn_bias_grad, ("seq", "batch"), scatter_dimension=0, tiled=True),
-        lax.psum_scatter(chan_gain_grad, ("seq", "batch"), scatter_dimension=0, tiled=True),
-        lax.psum_scatter(chan_bias_grad, ("seq", "batch"), scatter_dimension=0, tiled=True),
-        lax.psum_scatter(key_ratio_grad, ("seq", "batch"), scatter_dimension=0, tiled=True),
-        lax.psum_scatter(value_ratio_grad, ("seq", "batch"), scatter_dimension=0, tiled=True),
-        lax.psum_scatter(gate_ratio_grad, ("seq", "batch"), scatter_dimension=0, tiled=True),
-        lax.psum_scatter(expand_ratio_grad, ("seq", "batch"), scatter_dimension=0, tiled=True),
-        lax.psum_scatter(select_ratio_grad, ("seq", "batch"), scatter_dimension=0, tiled=True),
-        lax.psum_scatter(decay_grad, ("seq", "batch"), scatter_dimension=0, tiled=True),
-        lax.psum_scatter(present_reward_adjoint, ("seq", "batch"), scatter_dimension=0, tiled=True),
+        lax.psum_scatter(key_grad, BOTH, scatter_dimension=0, tiled=True),
+        lax.psum_scatter(value_grad, BOTH, scatter_dimension=0, tiled=True),
+        lax.psum_scatter(gate_grad, BOTH, scatter_dimension=0, tiled=True),
+        lax.psum_scatter(output_grad, BOTH, scatter_dimension=0, tiled=True),
+        lax.psum_scatter(expand_grad, BOTH, scatter_dimension=0, tiled=True),
+        lax.psum_scatter(select_grad, BOTH, scatter_dimension=0, tiled=True),
+        lax.psum_scatter(contract_grad, BOTH, scatter_dimension=0, tiled=True),
+        lax.psum_scatter(attn_gain_grad, BOTH, scatter_dimension=0, tiled=True),
+        lax.psum_scatter(attn_bias_grad, BOTH, scatter_dimension=0, tiled=True),
+        lax.psum_scatter(chan_gain_grad, BOTH, scatter_dimension=0, tiled=True),
+        lax.psum_scatter(chan_bias_grad, BOTH, scatter_dimension=0, tiled=True),
+        lax.psum_scatter(key_ratio_grad, BOTH, scatter_dimension=0, tiled=True),
+        lax.psum_scatter(value_ratio_grad, BOTH, scatter_dimension=0, tiled=True),
+        lax.psum_scatter(gate_ratio_grad, BOTH, scatter_dimension=0, tiled=True),
+        lax.psum_scatter(expand_ratio_grad, BOTH, scatter_dimension=0, tiled=True),
+        lax.psum_scatter(select_ratio_grad, BOTH, scatter_dimension=0, tiled=True),
+        lax.psum_scatter(decay_grad, BOTH, scatter_dimension=0, tiled=True),
+        lax.psum_scatter(present_reward_adjoint, BOTH, scatter_dimension=0, tiled=True),
     )
     return (
         block_out,
@@ -374,53 +1484,54 @@
 
 
 def solution(mesh):
+    fits = mesh.shape["seq"] == 8 and mesh.shape["batch"] == 4
     return jax.shard_map(
-        body,
+        fast_body if fits else body,
         mesh=mesh,
         in_specs=(
             P("batch", "seq", None),
             P("batch", "seq"),
-            P(("seq", "batch"), None),
-            P(("seq", "batch"), None),
-            P(("seq", "batch"), None),
-            P(("seq", "batch"), None),
-            P(("seq", "batch"), None),
-            P(("seq", "batch"), None),
-            P(("seq", "batch"), None),
-            P(("seq", "batch")),
-            P(("seq", "batch")),
-            P(("seq", "batch")),
-            P(("seq", "batch")),
-            P(("seq", "batch")),
-            P(("seq", "batch")),
-            P(("seq", "batch")),
-            P(("seq", "batch")),
-            P(("seq", "batch")),
-            P(("seq", "batch")),
-            P(("seq", "batch")),
+            P(BOTH, None),
+            P(BOTH, None),
+            P(BOTH, None),
+            P(BOTH, None),
+            P(BOTH, None),
+            P(BOTH, None),
+            P(BOTH, None),
+            P(BOTH),
+            P(BOTH),
+            P(BOTH),
+            P(BOTH),
+            P(BOTH),
+            P(BOTH),
+            P(BOTH),
+            P(BOTH),
+            P(BOTH),
+            P(BOTH),
+            P(BOTH),
             P("batch", "seq", None),
         ),
         out_specs=(
             P("batch", "seq", None),
             P("batch", "seq", None),
-            P(("seq", "batch"), None),
-            P(("seq", "batch"), None),
-            P(("seq", "batch"), None),
-            P(("seq", "batch"), None),
-            P(("seq", "batch"), None),
-            P(("seq", "batch"), None),
-            P(("seq", "batch"), None),
-            P(("seq", "batch")),
-            P(("seq", "batch")),
-            P(("seq", "batch")),
-            P(("seq", "batch")),
-            P(("seq", "batch")),
-            P(("seq", "batch")),
-            P(("seq", "batch")),
-            P(("seq", "batch")),
-            P(("seq", "batch")),
-            P(("seq", "batch")),
-            P(("seq", "batch")),
+            P(BOTH, None),
+            P(BOTH, None),
+            P(BOTH, None),
+            P(BOTH, None),
+            P(BOTH, None),
+            P(BOTH, None),
+            P(BOTH, None),
+            P(BOTH),
+            P(BOTH),
+            P(BOTH),
+            P(BOTH),
+            P(BOTH),
+            P(BOTH),
+            P(BOTH),
+            P(BOTH),
+            P(BOTH),
+            P(BOTH),
+            P(BOTH),
         ),
         check_vma=False,
     )

time: 1970 us -> 320 us (0.16); the launches traced: 1940 us -> 320 us
  local copies, waits for them, and re-layouts: 775 us -> 12.3 us
  waiting for transfers between devices: 589 us -> 0 us
  Pallas kernels: 0 us -> 305 us
  other arithmetic: 255 us -> 2.03 us
  blocking collectives: 169 us -> 0 us
  matrix products: 122 us -> 0 us
    reduce_scatter x7 -> x0, waiting for transfers between devices: 584 us -> none  [the longest x1 142 us: body(): lax.psum_scatter(expand_grad, ('seq', 'batch'), scatter_dimension=0, tile...]
    slice x166 -> x2, local copies, waits for them, and re-layouts: 555 us -> 1.47 us  [the longest x1 0.74 us: fast_body(): out[104:128]]
    pallas_call x0 -> x2, Pallas kernels: none -> 305 us  [the longest x1 177 us: backward_call(): pl.pallas_call(backward_kernel, out_shape=(s((rows, WIDE), F32), s((TOK,...]
    pad x56 -> x0, local copies, waits for them, and re-layouts: 170 us -> none  [the longest x28 89.1 us: forward_sweep(): lax.associative_scan(affine_compose, (multiplier, exponentiated_lookup *...]
    add x72 -> x0, other arithmetic: 144 us -> none  [the longest x15 40.1 us: affine_compose(): second_mult * first_numer + second_numer]
    dot_general x21 -> x0, matrix products: 122 us -> none  [the longest x7 52.1 us: product(): jnp.einsum('scd,de->sce', left, right, preferred_element_type=jnp.float32)]
    unnamed x3 -> x0, blocking collectives: 99.4 us -> none
    all_gather x4 -> x0, blocking collectives: 69.4 us -> none  [prefix(): gathered = jax.tree.map(lambda a: lax.all_gather(a, axis), part)]
  transfers between devices with their start and end apart: 18 -> 0, of which waited for: 6 -> 0; matrix products, arithmetic and copies ran while one was open for 57% -> 0% of each run, Pallas kernels for 0% -> 0%
where the time goes in v1:
time: 320 us
  Pallas kernels  305 us (95%)
  local copies, waits for them, and re-layouts  12.3 us (4%)
    pallas_call x1, Pallas kernels, backward_call(): pl.pallas_call(backward_kernel, out_shape=(s((rows, WIDE), F32), s((TOK,...  177 us
    pallas_call x1, Pallas kernels, forward_call(): pl.pallas_call(forward_kernel, out_shape=tuple(outs.values()), in_specs=[...  128 us
    transpose x2, local copies, waits for them, and re-layouts, natural(): v.reshape(SEQS, STEPS, SEG, WIDE).transpose(0, 2, 1, 3)  7.5 us

profile of v1, /device:TPU:0, one launch (start us, length us, event | category | flops | bytes accessed | tf_op | source)
XLA Modules:
  0.0 319.8 jit_solution(3360523308960981828)
XLA Ops:
  0.7 0.7 convert_subtract_fusion
  1.3 1.5 stack.47
  2.9 0.6 pad_convert_fusion.vec_in
  3.5 0.1 reshape.64
  3.5 0.1 copy.43
  3.6 0.1 broadcast_in_dim.7
  3.7 1.0 broadcast_in_dim.8.keep_in.i_keep
  4.7 127.8 %shard_map.356 = (bf16[5,768,768]{2,1,0:T(8,128)(2,1)}, bf16[4,768,768]{2,1,0:T(8,128)(2,1)}, bf16[4,2,4,96,768]{4,3,2,1,0:T(8,128)(2,1)}, bf16[3,1024,768]{2,1,...) custom-call(bf16[1024,768]{1,0:T(8,128)(2,1)} %bitcast.60, ...), custom_call_target="tpu_custom_call" | custom-call | flops 14495514624 | bytes 62914560 | tf_op jit(solution)/shard_map/pallas_call | solution.py:640
  132.5 2.9 copy.44
  135.4 176.9 %shard_map.357 = (f32[320,768]{1,0:T(8,128)}, f32[1024,768]{1,0:T(8,128)}, f32[16,128]{1,0:T(8,128)}) custom-call(bf16[5,768,768]{2,1,0:T(8,128)(2,1)} %get-tuple-element.45.i_w, bf16[4,768,768]{2,1,0:T(8,128)(2,1)} %get-tuple-element.46.i_e, bf16[4,2,4,96,768]{4,3,2,1,0:T(8,128)(2,1)} %get-tuple-element.47.i_c, ...), custom_call_target="tpu_custom_call" | custom-call | flops 31406948352 | bytes 62914560 | tf_op jit(solution)/shard_map/pallas_call | solution.py:1079
  312.4 0.0 copy-start.1
  312.4 0.0 copy-start
  312.4 4.6 %copy.45 = f32[4,8,32,768]{3,2,1,0:T(8,128)} copy(f32[4,8,32,768]{3,1,2,0:T(8,128)} %bitcast.45) | data formatting | bytes 6291456 | tf_op jit(solution)/shard_map/transpose | solution.py:1112
  317.0 0.0 copy-done.1
  317.0 0.6 slice_bitcast_fusion
  317.6 0.0 copy-done
  317.6 0.7 slice.72
  318.3 0.7 fusion
  319.0 0.7 pad_maximum_fusion
Async XLA Ops:
  312.4 4.6 %copy-start.1 = (f32[16,128]{1,0:T(8,128)S(1)}, f32[16,128]{1,0:T(8,128)}, u32[]{:S(2)}) copy-start(f32[16,128]{1,0:T(8,128)} %get-tuple-element.67) | copy-start | bytes 24580
  312.4 5.2 %copy-start = (f32[320,768]{1,0:T(8,128)S(1)}, f32[320,768]{1,0:T(8,128)}, u32[]{:S(2)}) copy-start(f32[320,768]{1,0:T(8,128)} %get-tuple-element.66) | copy-start | bytes 2949124
